TPU v7x, 512 devices: a whole 4x4x16 slice. The times are simulated.
512 devices in a mesh: slab: 64 (over z, x), col: 8 (over y, core).
Axes of the slice: x: 4, y: 4, z: 16, core: 2. Of those that a mesh axis runs over, the one named last changes fastest.
Arguments:
- rhs: float32 [64, 262144], P(None, ('slab', 'col')), may hold values from -6 to 6
- start: float32 [64, 262144], P(None, ('slab', 'col')), may hold values from -4 to 4
- screen: float32 [64, 262144], P(None, ('slab', 'col')), may hold values from 0.2 to 5
- neighbours: int32 [27, 262144], P(None, ('slab', 'col')), may hold values from 0 to 1088, as said below
- col_send: int32 [2, 65536], P(None, ('slab', 'col')), may hold values from 0 to 512, as said below
- slab_send: int32 [2, 81920], P(None, ('slab', 'col')), may hold values from 0 to 768
- coarse_map: int32 [262144], P(('slab', 'col')), may hold values from 0 to 15
- coupling: float32 [128, 16, 4], P('slab', 'col'), may hold values from 0.1 to 1
- coarse_scale: float32 [128, 16, 4], P('slab', 'col'), may hold values from 0.05 to 0.2
Outputs:
- solution: float32 [64, 262144], P(None, ('slab', 'col'))
Inputs may be any that keep to these rules, and one draw needn't show every extreme that they name: `neighbours`: indices into the extended brick list; index 512 is the zero brick, and offsets that leave the strip's height point to it. `col_send`: each block holds exactly 512 occupied bricks, in the order of their positions; its eight corner positions are always occupied.
All inputs are finite; a program needn't handle non-finite values.
Results may differ from a plain program's by a relative error of at most 0.0003.
Values sent between devices are 32-bit elements; how exact they have to be, the bound alone decides.
A program may use at most 64 MiB of HBM per device.

v0:
```python
import jax
import jax.numpy as jnp
import numpy as np
from jax import lax
from jax.sharding import PartitionSpec as P

SWEEPS = 2
CX = 2
CY = 2
CZ = 4
CELLS = 16


relax_weight = 0.5


def with_halo(cells, sides, width):
    for axis, dim in sides:
        count = lax.axis_size(axis)
        ends = count - 1
        head = lax.slice_in_dim(cells, 0, width, axis=dim)
        tail = lax.slice_in_dim(cells, cells.shape[dim] - width, cells.shape[dim], axis=dim)
        cells = jnp.concatenate(
            [
                lax.ppermute(tail, axis, [(i, (i + 1) % count) for i in range(ends)]),
                cells,
                lax.ppermute(head, axis, [((i + 1) % count, i) for i in range(ends)]),
            ],
            axis=dim,
        )
    return cells


def carried_in(array, axis, combine, identity, reverse):
    length, place = (lax.axis_size(axis), lax.axis_index(axis))
    everything = jax.tree.map(lambda part: lax.all_gather(part, axis), array)
    start = jax.tree.map(
        lambda part, zero: jnp.broadcast_to(jnp.asarray(zero, part.dtype), part.shape),
        array,
        identity,
    )

    def turn(k, before):
        at = length - 1 - k if reverse else k
        reached = at > place if reverse else at < place
        new = combine(before, jax.tree.map(lambda part: part[at], everything))
        return jax.tree.map(lambda a, b: jnp.where(reached, a, b), new, before)

    return lax.fori_loop(0, length, turn, start)


def stencil_table():
    masses = np.array([11.0 / 20.0, 13.0 / 60.0, 1.0 / 120.0])
    slopes = np.array([1.0, -1.0 / 3.0, -1.0 / 6.0])
    coeffs = np.arange(64)
    along_x = coeffs // 16
    along_y = coeffs // 4 % 4
    along_z = coeffs % 4
    offsets = np.arange(27)
    shift_x = offsets // 9 - 1
    shift_y = offsets // 3 % 3 - 1
    shift_z = offsets % 3 - 1
    dist_x = 4 * shift_x[None, :, None] + along_x[None, None, :] - along_x[:, None, None]
    dist_y = 4 * shift_y[None, :, None] + along_y[None, None, :] - along_y[:, None, None]
    dist_z = 4 * shift_z[None, :, None] + along_z[None, None, :] - along_z[:, None, None]
    inside = (np.abs(dist_x) <= 2) & (np.abs(dist_y) <= 2) & (np.abs(dist_z) <= 2)
    mass_x = masses[np.minimum(np.abs(dist_x), 2)]
    mass_y = masses[np.minimum(np.abs(dist_y), 2)]
    mass_z = masses[np.minimum(np.abs(dist_z), 2)]
    slope_x = slopes[np.minimum(np.abs(dist_x), 2)]
    slope_y = slopes[np.minimum(np.abs(dist_y), 2)]
    slope_z = slopes[np.minimum(np.abs(dist_z), 2)]
    values = slope_x * mass_y * mass_z + mass_x * slope_y * mass_z + mass_x * mass_y * slope_z
    return np.where(inside, values, 0.0).astype(np.float32)


def compose(earlier, later):
    return (earlier[0] * later[0], later[0] * earlier[1] + later[1])


def grow(extended_faces):
    lower = extended_faces[:, 0]
    upper = extended_faces[:, 3]
    return (lower, upper)


def widen(base_cols, col_send, slab_send):
    col_buffer = jnp.stack(
        [jnp.take(base_cols, col_send[0], axis=1), jnp.take(base_cols, col_send[1], axis=1)], axis=1
    )
    col_ext = with_halo(col_buffer, (("col", 1),), 1)
    col_lower, col_upper = grow(col_ext)
    widened = jnp.concatenate([base_cols, col_lower, col_upper], axis=1)
    slab_buffer = jnp.stack(
        [jnp.take(widened, slab_send[0], axis=1), jnp.take(widened, slab_send[1], axis=1)], axis=1
    )
    slab_ext = with_halo(slab_buffer, (("slab", 1),), 1)
    slab_lower, slab_upper = grow(slab_ext)
    return jnp.concatenate([widened, slab_lower, slab_upper], axis=1)


def shards(rhs, start, screen, neighbours, col_send, slab_send, coarse_map, coupling, coarse_scale):
    table_np = stencil_table()
    stencil = jnp.asarray(table_np)
    centre = float(table_np[0, 13, 0])
    bricks = rhs.shape[1]
    diagonal = centre + screen

    def operate(field):
        base_cols = jnp.concatenate([field, jnp.zeros((64, 1), jnp.float32)], axis=1)
        extended = widen(base_cols, col_send, slab_send)
        total = screen * field
        for offset_group in range(3):
            index = neighbours[9 * offset_group : 9 * offset_group + 9].reshape(-1)
            gathered = jnp.take(extended, index, axis=1).reshape(64, 9, bricks)
            total = total + jnp.einsum(
                "ioj,jon->in",
                stencil[:, 9 * offset_group : 9 * offset_group + 9],
                gathered,
                precision=lax.Precision.HIGHEST,
            )
        return total

    field = start
    for sweep in range(SWEEPS):
        field = field + relax_weight * (rhs - operate(field)) / diagonal
    residual = rhs - operate(field)
    onehot = (coarse_map[None, :] == jnp.arange(CELLS, dtype=jnp.int32)[:, None]).astype(
        jnp.float32
    )
    brick_mean = jnp.sum(residual, axis=0) / 64.0
    coarse = jnp.dot(onehot, brick_mean, precision=lax.Precision.HIGHEST).reshape(CX, CY, CZ)
    gathered_rows = lax.all_gather(coarse, "col", axis=1, tiled=True)
    total_rows = gathered_rows.shape[1]
    eye_rows = jnp.eye(total_rows, dtype=jnp.float32)
    ymatrix = (
        2.5 * eye_rows
        - jnp.eye(total_rows, k=1, dtype=jnp.float32)
        - jnp.eye(total_rows, k=-1, dtype=jnp.float32)
    )
    factor = jnp.linalg.cholesky(ymatrix)
    inverse = jax.scipy.linalg.cho_solve((factor, True), eye_rows)
    own_rows = lax.dynamic_slice_in_dim(inverse, lax.axis_index("col") * CY, CY, 0)
    mixed = jnp.einsum("yk,xkz->xyz", own_rows, gathered_rows, precision=lax.Precision.HIGHEST)
    ones_line = jnp.ones((CY, CZ), jnp.float32)
    zero_line = jnp.zeros((CY, CZ), jnp.float32)
    product = ones_line
    offset_sum = zero_line
    for position in range(CX):
        product = coupling[position] * product
        offset_sum = coupling[position] * offset_sum + mixed[position]
    entering = carried_in((product, offset_sum), "slab", compose, (ones_line, zero_line), False)[1]
    lines = []
    state = entering
    for position in range(CX):
        state = mixed[position] + coupling[position] * state
        lines.append(state)
    product = ones_line
    offset_sum = zero_line
    for position in reversed(range(CX)):
        product = coupling[position] * product
        offset_sum = coupling[position] * offset_sum + coarse_scale[position] * lines[position]
    leaving = carried_in((product, offset_sum), "slab", compose, (ones_line, zero_line), True)[1]
    pieces = [None] * CX
    state = leaving
    for position in reversed(range(CX)):
        state = coarse_scale[position] * lines[position] + coupling[position] * state
        pieces[position] = state
    correction = jnp.stack(pieces, axis=0)
    per_brick = jnp.dot(correction.reshape(-1), onehot, precision=lax.Precision.HIGHEST)
    return field + per_brick[None, :]


def solution(mesh):
    placed = (
        P(None, ("slab", "col")),
        P(None, ("slab", "col")),
        P(None, ("slab", "col")),
        P(None, ("slab", "col")),
        P(None, ("slab", "col")),
        P(None, ("slab", "col")),
        P(("slab", "col")),
        P("slab", "col", None),
        P("slab", "col", None),
    )
    return jax.shard_map(
        shards, mesh=mesh, in_specs=placed, out_specs=P(None, ("slab", "col")), check_vma=False
    )
```

profile of v0, /device:TPU:2, one launch (start us, length us, event | category | flops | bytes accessed | tf_op | source)
XLA Modules:
  0.0 465.3 jit_solution(13482977044275830617)
XLA Ops:
  2.6 1.7 collective-permute-start
  10.8 3.4 collective-permute-start.2
  15.0 5.3 %collective-permute-start.3 = (f32[64,1,160]{0,2,1:T(8,128)S(1)}, f32[64,1,160]{0,2,1:T(8,128)S(1)}, u32[]{:S(2)}, u32[]{:S(2)}) collective-permute-start(f32[64,1,160]{0,2,1:T(8,128)S(1)} %select_bitcast_fusion), channel_id=1, source_target_pairs={{8,0},{16,8},{24,16},{32,24},{40,32},{48,40},{56,48},{64,56},{72,6... | collective-permute-start | bytes 122888 | tf_op jit(solution)/shard_map/ppermute | solution.py:27
  20.8 2.1 collective-permute-done.3
  23.9 9.3 %gather_fusion.6 = f32[4608,64]{1,0:T(8,128)} fusion(f32[64,1089]{0,1:T(8,128)S(1)} %concatenate.35, s32[5120]{0:T(1024)S(1)} %pad_clamp_fusion), kind=kCustom, calls=%fused_computation.14.clone | custom fusion | bytes 2377728 | tf_op jit(solution)/shard_map/jit(_take)/gather | solution.py:115
  33.2 9.3 %gather_fusion.5 = f32[4608,64]{1,0:T(8,128)} fusion(f32[64,1089]{0,1:T(8,128)S(1)} %concatenate.35, s32[5120]{0:T(1024)S(1)} %pad_clamp_fusion.1), kind=kCustom, calls=%fused_computation.13.clone | custom fusion | bytes 2377728 | tf_op jit(solution)/shard_map/jit(_take)/gather | solution.py:115
  42.5 7.2 %gather_fusion.4 = f32[4608,64]{1,0:T(8,128)S(1)} fusion(f32[64,1089]{0,1:T(8,128)S(1)} %concatenate.35, s32[5120]{0:T(1024)S(1)} %pad_clamp_fusion.2), kind=kCustom, calls=%fused_computation.2.clone | custom fusion | bytes 2377728 | tf_op jit(solution)/shard_map/jit(_take)/gather | solution.py:115
  49.8 3.9 broadcast_select_fusion.6
  53.6 2.3 convolution_bitcast_fusion.6
  56.0 2.4 broadcast_select_fusion.7
  58.4 2.3 convolution_bitcast_fusion.7
  60.8 2.4 broadcast_select_fusion.8
  63.3 2.3 fusion.8
  67.3 2.3 collective-permute-start.4
  71.7 2.9 collective-permute-done.5
  76.5 3.1 collective-permute-start.6
  79.7 2.9 collective-permute-start.7
  83.3 1.8 custom-call.10
  85.2 2.6 collective-permute-done.7
  88.2 9.3 %gather_fusion.13 = f32[4608,64]{1,0:T(8,128)} fusion(f32[64,1089]{0,1:T(8,128)S(1)} %copy.60, s32[5120]{0:T(1024)S(1)} %pad_clamp_fusion), kind=kCustom, calls=%fused_computation.17.clone | custom fusion | bytes 2377728 | tf_op jit(solution)/shard_map/jit(_take)/gather | solution.py:115
  97.4 9.3 %gather_fusion.12 = f32[4608,64]{1,0:T(8,128)} fusion(f32[64,1089]{0,1:T(8,128)S(1)} %copy.60, s32[5120]{0:T(1024)S(1)} %pad_clamp_fusion.1), kind=kCustom, calls=%fused_computation.16.clone | custom fusion | bytes 2377728 | tf_op jit(solution)/shard_map/jit(_take)/gather | solution.py:115
  106.7 7.2 %gather_fusion.11 = f32[4608,64]{1,0:T(8,128)S(1)} fusion(f32[64,1089]{0,1:T(8,128)S(1)} %copy.60, s32[5120]{0:T(1024)S(1)} %pad_clamp_fusion.2), kind=kCustom, calls=%fused_computation.15.clone | custom fusion | bytes 2377728 | tf_op jit(solution)/shard_map/jit(_take)/gather | solution.py:115
  114.0 3.9 broadcast_select_fusion.3
  117.9 2.3 convolution_bitcast_fusion.3
  120.2 2.4 broadcast_select_fusion.4
  122.7 2.3 convolution_bitcast_fusion.4
  125.0 2.4 broadcast_select_fusion.5
  127.5 2.3 fusion.15
  131.6 3.4 collective-permute-start.8
  136.6 2.3 collective-permute-done.9
  140.8 4.3 collective-permute-start.10
  145.2 2.1 collective-permute-start.11
  148.1 3.3 collective-permute-done.11
  151.7 9.3 %gather_fusion.20 = f32[4608,64]{1,0:T(8,128)} fusion(f32[64,1089]{0,1:T(8,128)S(1)} %copy.74, s32[5120]{0:T(1024)S(1)} %pad_clamp_fusion), kind=kCustom, calls=%fused_computation.20.clone | custom fusion | bytes 2377728 | tf_op jit(solution)/shard_map/jit(_take)/gather | solution.py:115
  161.0 9.3 %gather_fusion.19 = f32[4608,64]{1,0:T(8,128)} fusion(f32[64,1089]{0,1:T(8,128)S(1)} %copy.74, s32[5120]{0:T(1024)S(1)} %pad_clamp_fusion.1), kind=kCustom, calls=%fused_computation.19.clone | custom fusion | bytes 2377728 | tf_op jit(solution)/shard_map/jit(_take)/gather | solution.py:115
  170.3 7.2 %gather_fusion.18 = f32[4608,64]{1,0:T(8,128)S(1)} fusion(f32[64,1089]{0,1:T(8,128)S(1)} %copy.74, s32[5120]{0:T(1024)S(1)} %copy-done.18), kind=kCustom, calls=%fused_computation.18.clone | custom fusion | bytes 2377728 | tf_op jit(solution)/shard_map/jit(_take)/gather | solution.py:115
  177.5 3.9 broadcast_select_fusion
  181.4 2.3 convolution_bitcast_fusion
  183.8 2.4 broadcast_select_fusion.1
  186.2 2.3 convolution_bitcast_fusion.1
  188.6 2.4 broadcast_select_fusion.2
  191.1 2.3 fusion.20
  193.6 13.9 %all_gather.19 = f32[2,16,4]{2,0,1:T(2,128)S(1)} all-gather(f32[2,2,4]{2,0,1:T(2,128)S(1)} %copy.77), channel_id=1, replica_groups=mesh['slab'=64,'col'=8] {'col'}, dimensions={1}, use_global_device_ids=true | all-gather | bytes 576 | tf_op jit(solution)/shard_map/all_gather | solution.py:133
  208.4 90.8 %all_gather.20 = f32[64,2,4]{2,1,0:T(2,128)S(1)} all-gather(f32[1,2,4]{2,1,0:T(2,128)S(1)} %get-tuple-element.305), channel_id=1, replica_groups=mesh['slab'=64,'col'=8] {'slab'}, dimensions={0}, use_global_device_ids=true | all-gather | bytes 2080 | tf_op jit(solution)/shard_map/all_gather | solution.py:36
  299.1 78.3 %all_gather.21 = f32[64,2,4]{2,1,0:T(2,128)S(1)} all-gather(f32[1,2,4]{2,1,0:T(2,128)S(1)} %get-tuple-element.304), channel_id=1, replica_groups=mesh['slab'=64,'col'=8] {'slab'}, dimensions={0}, use_global_device_ids=true | all-gather | bytes 2080 | tf_op jit(solution)/shard_map/all_gather | solution.py:36
  377.5 2.5 while.30
  380.0 81.5 %all-gather.1 = f32[64,2,4]{2,1,0:T(2,128)S(1)} all-gather(f32[1,2,4]{2,1,0:T(2,128)S(1)} %get-tuple-element.292), channel_id=2, replica_groups=mesh['slab'=64,'col'=8] {'slab'}, dimensions={0}, use_global_device_ids=true | all-gather | bytes 2080 | tf_op jit(solution)/shard_map/all_gather | solution.py:36
  461.5 2.8 while.31
  (335 shorter events, 28.4 us)
Async XLA Ops:
  1.8 22.1 %copy-start.34 = (pred[128]{0:T(512)(128)(4,1)}, pred[128]{0:T(512)(128)(4,1)S(1)}, u32[]{:S(2)}) copy-start(pred[128]{0:T(512)(128)(4,1)S(1)} %get-tuple-element.295) | copy-start | bytes 388
  1.8 22.1 %copy-start.37 = (pred[128]{0:T(512)(128)(4,1)}, pred[128]{0:T(512)(128)(4,1)S(1)}, u32[]{:S(2)}) copy-start(pred[128]{0:T(512)(128)(4,1)S(1)} %get-tuple-element.308) | copy-start | bytes 388
  1.8 64.0 %copy-start.40 = (s32[1024]{0:T(1024)}, s32[1024]{0:T(1024)S(1)}, u32[]{:S(2)}) copy-start(s32[1024]{0:T(1024)S(1)} %pad_clamp_fusion.6) | copy-start | bytes 12292
  2.6 7.3 %collective-permute-start = (f32[64,1,128]{0,2,1:T(8,128)S(1)}, f32[64,1,128]{0,2,1:T(8,128)S(1)}, u32[]{:S(2)}, u32[]{:S(2)}) collective-permute-start(f32[64,1,128]{0,2,1:T(8,128)S(1)} %select_bitcast_fusion.7), channel_id=1, source_target_pairs={{0,1},{1,2},{2,3},{3,4},{4,5},{5,6},{6,7},{8,9},{9,10},{10,11},{11... | collective-permute-start | bytes 98312 | tf_op jit(solution)/shard_map/ppermute | solution.py:25
  4.4 3.8 copy-start.41
  5.1 4.8 %collective-permute-start.1 = (f32[64,1,128]{0,2,1:T(8,128)S(1)}, f32[64,1,128]{0,2,1:T(8,128)S(1)}, u32[]{:S(2)}, u32[]{:S(2)}) collective-permute-start(f32[64,1,128]{0,2,1:T(8,128)S(1)} %select_bitcast_fusion.6), channel_id=1, source_target_pairs={{1,0},{2,1},{3,2},{4,3},{5,4},{6,5},{7,6},{9,8},{10,9},{11,10},{12... | collective-permute-start | bytes 98312 | tf_op jit(solution)/shard_map/ppermute | solution.py:27
  7.2 26.0 %copy-start.45 = (pred[160]{0:T(512)(128)(4,1)}, pred[160]{0:T(512)(128)(4,1)S(1)}, u32[]{:S(2)}) copy-start(pred[160]{0:T(512)(128)(4,1)S(1)} %compare_and_fusion.4) | copy-start | bytes 484
  7.2 26.0 %copy-start.42 = (pred[160]{0:T(512)(128)(4,1)}, pred[160]{0:T(512)(128)(4,1)S(1)}, u32[]{:S(2)}) copy-start(pred[160]{0:T(512)(128)(4,1)S(1)} %compare_and_fusion.3) | copy-start | bytes 484
  8.2 41.5 %copy-start.25 = (pred[4608]{0:T(1024)(128)(4,1)}, pred[4608]{0:T(1024)(128)(4,1)S(1)}, u32[]{:S(2)}) copy-start(pred[4608]{0:T(1024)(128)(4,1)S(1)} %compare_and_fusion) | copy-start | bytes 13828
  8.2 47.7 %copy-start.19 = (pred[4608]{0:T(1024)(128)(4,1)}, pred[4608]{0:T(1024)(128)(4,1)S(1)}, u32[]{:S(2)}) copy-start(pred[4608]{0:T(1024)(128)(4,1)S(1)} %compare_and_fusion.1) | copy-start | bytes 13828
  8.3 52.4 %copy-start.22 = (pred[4608]{0:T(1024)(128)(4,1)}, pred[4608]{0:T(1024)(128)(4,1)S(1)}, u32[]{:S(2)}) copy-start(pred[4608]{0:T(1024)(128)(4,1)S(1)} %compare_and_fusion.2) | copy-start | bytes 13828
  8.4 98.3 %copy-start.17 = (s32[5120]{0:T(1024)}, s32[5120]{0:T(1024)S(1)}, u32[]{:S(2)}) copy-start(s32[5120]{0:T(1024)S(1)} %pad_clamp_fusion.2) | copy-start | bytes 61444
  8.5 24.7 %copy-start.33 = (s32[1024]{0:T(1024)}, s32[1024]{0:T(1024)S(1)}, u32[]{:S(2)}) copy-start(s32[1024]{0:T(1024)S(1)} %pad_clamp_fusion.3) | copy-start | bytes 12292
  9.9 23.3 %copy-start.30 = (f32[16,16]{1,0:T(8,128)}, f32[16,16]{1,0:T(8,128)S(1)}, u32[]{:S(2)}) copy-start(f32[16,16]{1,0:T(8,128)S(1)} %cholesky.17) | copy-start | bytes 3076
  10.8 10.0 %collective-permute-start.2 = (f32[64,1,160]{0,2,1:T(8,128)S(1)}, f32[64,1,160]{0,2,1:T(8,128)S(1)}, u32[]{:S(2)}, u32[]{:S(2)}) collective-permute-start(f32[64,1,160]{0,2,1:T(8,128)S(1)} %select_bitcast_fusion.1), channel_id=1, source_target_pairs={{0,8},{8,16},{16,24},{24,32},{32,40},{40,48},{48,56},{56,64},{64,7... | collective-permute-start | bytes 122888 | tf_op jit(solution)/shard_map/ppermute | solution.py:25
  15.0 7.9 %collective-permute-start.3 = (f32[64,1,160]{0,2,1:T(8,128)S(1)}, f32[64,1,160]{0,2,1:T(8,128)S(1)}, u32[]{:S(2)}, u32[]{:S(2)}) collective-permute-start(f32[64,1,160]{0,2,1:T(8,128)S(1)} %select_bitcast_fusion), channel_id=1, source_target_pairs={{8,0},{16,8},{24,16},{32,24},{40,32},{48,40},{56,48},{64,56},{72,6... | collective-permute-start | bytes 122888 | tf_op jit(solution)/shard_map/ppermute | solution.py:27
  49.7 3.9 copy-start.7
  60.7 2.5 copy-start.3
  60.7 2.5 copy-start.10
  63.3 4.0 copy-start.38
  63.3 6.4 %copy-start.35 = (pred[128]{0:T(512)(128)(4,1)S(1)}, pred[128]{0:T(512)(128)(4,1)}, u32[]{:S(2)}) copy-start(pred[128]{0:T(512)(128)(4,1)} %copy-done.34) | copy-start | bytes 388
  63.3 7.7 %copy-start.49 = (f32[16]{0:T(128)S(1)}, f32[16]{0:T(128)}, u32[]{:S(2)}) copy-start(f32[16]{0:T(128)} %select_reduce_fusion) | copy-start | bytes 196
  65.6 10.8 %copy-start.46 = (pred[160]{0:T(512)(128)(4,1)S(1)}, pred[160]{0:T(512)(128)(4,1)}, u32[]{:S(2)}) copy-start(pred[160]{0:T(512)(128)(4,1)} %copy-done.45) | copy-start | bytes 484
  65.6 14.0 %copy-start.43 = (pred[160]{0:T(512)(128)(4,1)S(1)}, pred[160]{0:T(512)(128)(4,1)}, u32[]{:S(2)}) copy-start(pred[160]{0:T(512)(128)(4,1)} %copy-done.42) | copy-start | bytes 484
  65.6 17.0 %copy-start.31 = (f32[16,16]{1,0:T(8,128)S(1)}, f32[16,16]{1,0:T(8,128)}, u32[]{:S(2)}) copy-start(f32[16,16]{1,0:T(8,128)} %copy-done.30) | copy-start | bytes 3076
  67.3 4.4 collective-permute-start.4
  69.7 4.9 %collective-permute-start.5 = (f32[64,1,128]{2,0,1:T(8,128)S(1)}, f32[64,1,128]{2,0,1:T(8,128)S(1)}, u32[]{:S(2)}, u32[]{:S(2)}) collective-permute-start(f32[64,1,128]{2,0,1:T(8,128)S(1)} %select_bitcast_fusion.10), channel_id=1, source_target_pairs={{1,0},{2,1},{3,2},{4,3},{5,4},{6,5},{7,6},{9,8},{10,9},{11,10},{12... | collective-permute-start | bytes 98312 | tf_op jit(solution)/shard_map/ppermute | solution.py:27
  76.5 8.7 %collective-permute-start.6 = (f32[64,1,160]{2,0,1:T(8,128)S(1)}, f32[64,1,160]{2,0,1:T(8,128)S(1)}, u32[]{:S(2)}, u32[]{:S(2)}) collective-permute-start(f32[64,1,160]{2,0,1:T(8,128)S(1)} %select_bitcast_fusion.5), channel_id=1, source_target_pairs={{0,8},{8,16},{16,24},{24,32},{32,40},{40,48},{48,56},{56,64},{64,7... | collective-permute-start | bytes 122888 | tf_op jit(solution)/shard_map/ppermute | solution.py:25
  79.7 8.1 %collective-permute-start.7 = (f32[64,1,160]{2,0,1:T(8,128)S(1)}, f32[64,1,160]{2,0,1:T(8,128)S(1)}, u32[]{:S(2)}, u32[]{:S(2)}) collective-permute-start(f32[64,1,160]{2,0,1:T(8,128)S(1)} %select_bitcast_fusion.4), channel_id=1, source_target_pairs={{8,0},{16,8},{24,16},{32,24},{40,32},{48,40},{56,48},{64,56},{72,6... | collective-permute-start | bytes 122888 | tf_op jit(solution)/shard_map/ppermute | solution.py:27
  106.7 7.3 %copy-start.26 = (pred[4608]{0:T(1024)(128)(4,1)S(1)}, pred[4608]{0:T(1024)(128)(4,1)}, u32[]{:S(2)}) copy-start(pred[4608]{0:T(1024)(128)(4,1)} %copy-done.25) | copy-start | bytes 13828
  114.0 3.9 copy-start.8
  127.5 4.1 copy-start.39
  127.5 7.6 %copy-start.36 = (pred[128]{0:T(512)(128)(4,1)S(1)}, pred[128]{0:T(512)(128)(4,1)}, u32[]{:S(2)}) copy-start(pred[128]{0:T(512)(128)(4,1)} %copy-done.34) | copy-start | bytes 388
  127.5 8.9 %copy-start.29 = (f32[1,16,16]{1,2,0:T(8,128)S(1)}, f32[1,16,16]{1,2,0:T(8,128)}, u32[]{:S(2)}) copy-start(f32[1,16,16]{1,2,0:T(8,128)} %custom-call.10) | copy-start | bytes 3076
  129.8 10.9 %copy-start.47 = (pred[160]{0:T(512)(128)(4,1)S(1)}, pred[160]{0:T(512)(128)(4,1)}, u32[]{:S(2)}) copy-start(pred[160]{0:T(512)(128)(4,1)} %copy-done.45) | copy-start | bytes 484
  129.8 15.3 %copy-start.44 = (pred[160]{0:T(512)(128)(4,1)S(1)}, pred[160]{0:T(512)(128)(4,1)}, u32[]{:S(2)}) copy-start(pred[160]{0:T(512)(128)(4,1)} %copy-done.42) | copy-start | bytes 484
  131.6 5.0 %collective-permute-start.8 = (f32[64,1,128]{2,0,1:T(8,128)S(1)}, f32[64,1,128]{2,0,1:T(8,128)S(1)}, u32[]{:S(2)}, u32[]{:S(2)}) collective-permute-start(f32[64,1,128]{2,0,1:T(8,128)S(1)} %select_bitcast_fusion.9), channel_id=1, source_target_pairs={{0,1},{1,2},{2,3},{3,4},{4,5},{5,6},{6,7},{8,9},{9,10},{10,11},{11... | collective-permute-start | bytes 98312 | tf_op jit(solution)/shard_map/ppermute | solution.py:25
  135.1 3.8 collective-permute-start.9
  140.8 7.3 %collective-permute-start.10 = (f32[64,1,160]{2,0,1:T(8,128)S(1)}, f32[64,1,160]{2,0,1:T(8,128)S(1)}, u32[]{:S(2)}, u32[]{:S(2)}) collective-permute-start(f32[64,1,160]{2,0,1:T(8,128)S(1)} %select_bitcast_fusion.3), channel_id=1, source_target_pairs={{0,8},{8,16},{16,24},{24,32},{32,40},{40,48},{48,56},{56,64},{64,7... | collective-permute-start | bytes 122888 | tf_op jit(solution)/shard_map/ppermute | solution.py:25
  145.2 6.2 %collective-permute-start.11 = (f32[64,1,160]{2,0,1:T(8,128)S(1)}, f32[64,1,160]{2,0,1:T(8,128)S(1)}, u32[]{:S(2)}, u32[]{:S(2)}) collective-permute-start(f32[64,1,160]{2,0,1:T(8,128)S(1)} %select_bitcast_fusion.2), channel_id=1, source_target_pairs={{8,0},{16,8},{24,16},{32,24},{40,32},{48,40},{56,48},{64,56},{72,6... | collective-permute-start | bytes 122888 | tf_op jit(solution)/shard_map/ppermute | solution.py:27
  161.0 9.3 %copy-start.18 = (s32[5120]{0:T(1024)S(1)}, s32[5120]{0:T(1024)}, u32[]{:S(2)}) copy-start(s32[5120]{0:T(1024)} %copy-done.17) | copy-start | bytes 61444
  170.3 7.3 %copy-start.27 = (pred[4608]{0:T(1024)(128)(4,1)S(1)}, pred[4608]{0:T(1024)(128)(4,1)}, u32[]{:S(2)}) copy-start(pred[4608]{0:T(1024)(128)(4,1)} %copy-done.25) | copy-start | bytes 13828
  177.5 3.9 copy-start.9
  188.5 2.5 copy-start.12
  188.5 2.5 copy-start.15
  191.0 17.4 %copy-start.32 = (f32[2,2,4]{2,1,0:T(2,128)S(1)}, f32[2,2,4]{2,1,0:T(2,128)}, u32[]{:S(2)}) copy-start(f32[2,2,4]{2,1,0:T(2,128)} %param.27) | copy-start | bytes 196
  191.0 188.9 %copy-start.48 = (f32[2,2,4]{2,1,0:T(2,128)S(1)}, f32[2,2,4]{2,1,0:T(2,128)}, u32[]{:S(2)}) copy-start(f32[2,2,4]{2,1,0:T(2,128)} %param.28) | copy-start | bytes 196
  191.1 270.5 %copy-start.28 = (f32[2,4]{1,0:T(2,128)S(1)}, f32[2,4]{1,0:T(2,128)}, u32[]{:S(2)}) copy-start(f32[2,4]{1,0:T(2,128)} %custom-call.12) | copy-start | bytes 100
  (15 other events, 36.0 us)
where the time goes:
time: 466 us; the launch traced here: 465 us
  blocking collectives  265 us (57%)
  local copies, waits for them, and re-layouts  92 us (20%)
  other arithmetic  36 us (8%)
  starting transfers between devices  32.4 us (7%)
  matrix products  22.6 us (5%)
  waiting for transfers between devices  13.1 us (3%)
    all_gather x3, blocking collectives, carried_in(): everything = jax.tree.map(lambda part: lax.all_gather(part, axis), array)  251 us
    gather x9, local copies, waits for them, and re-layouts, operate(): gathered = jnp.take(extended, index, axis=1).reshape(64, 9, bricks)  77.4 us
    select_n x12, other arithmetic, operate(): gathered = jnp.take(extended, index, axis=1).reshape(64, 9, bricks)  26.3 us
    dot_general x9, matrix products, operate(): jnp.einsum('ioj,jon->in', stencil[:, 9 * offset_group:9 * offset_group +...  20.6 us
    ppermute x6, starting transfers between devices, with_halo(): lax.ppermute(tail, axis, [(i, (i + 1) % count) for i in range(ends)])  18.2 us
    ppermute x6, starting transfers between devices, with_halo(): lax.ppermute(head, axis, [((i + 1) % count, i) for i in range(ends)])  14.2 us
    all_gather x1, blocking collectives, shards(): gathered_rows = lax.all_gather(coarse, 'col', axis=1, tiled=True)  13.9 us
    ppermute x6, waiting for transfers between devices, with_halo(): lax.ppermute(head, axis, [((i + 1) % count, i) for i in range(ends)])  13.1 us
  transfers between devices with their start and end apart: 12, of which 5 were waited for; matrix products, arithmetic and copies ran while one was open for 2% of the time, Pallas kernels for 0%

commit v1 on v0

v1 whole, which is shorter than its diff:
```python
import functools

import jax
import jax.numpy as jnp
import numpy as np
from jax import lax
from jax.experimental import pallas as pl
from jax.experimental.pallas import tpu as pltpu
from jax.sharding import PartitionSpec as P

MESH = pl.DeviceIdType.MESH
F32 = jnp.float32
BF16 = jnp.bfloat16
I32 = jnp.int32
NB = 512
FCOL = 128
FSLAB = 160
RELAX = 0.5
COL0 = NB + 1
SLAB_LOW = COL0 + 2 * FCOL
SLAB_HIGH = SLAB_LOW + FSLAB
NOWHERE = -1000


def stencil_table():
    masses = np.array([11.0 / 20.0, 13.0 / 60.0, 1.0 / 120.0])
    slopes = np.array([1.0, -1.0 / 3.0, -1.0 / 6.0])
    coeffs = np.arange(64)
    along = (coeffs // 16, coeffs // 4 % 4, coeffs % 4)
    offsets = np.arange(27)
    shift = (offsets // 9 - 1, offsets // 3 % 3 - 1, offsets % 3 - 1)
    dist = [
        4 * shift[k][None, :, None] + along[k][None, None, :] - along[k][:, None, None]
        for k in range(3)
    ]
    inside = (np.abs(dist[0]) <= 2) & (np.abs(dist[1]) <= 2) & (np.abs(dist[2]) <= 2)
    m = [masses[np.minimum(np.abs(d), 2)] for d in dist]
    s = [slopes[np.minimum(np.abs(d), 2)] for d in dist]
    values = s[0] * m[1] * m[2] + m[0] * s[1] * m[2] + m[0] * m[1] * s[2]
    return np.where(inside, values, 0.0)


def split_np(x):
    x = np.asarray(x, np.float32)
    high = x.astype(jnp.bfloat16)
    return high, (x - high.astype(np.float32)).astype(jnp.bfloat16)


def tables(n_col):
    stencil = stencil_table()
    packed = np.zeros((64, 512))
    for blk in range(8):
        sx, sy, sz = blk // 4, blk // 2 % 2, blk % 2
        for j in range(64):
            a, b, e = j // 16, j // 4 % 4, j % 4
            dx = sx * (1 if a < 2 else -1)
            dy = sy * (1 if b < 2 else -1)
            dz = sz * (1 if e < 2 else -1)
            packed[:, blk * 64 + j] = stencil[:, 9 * (dx + 1) + 3 * (dy + 1) + dz + 1, j]
    stack = np.concatenate(split_np(packed), 0)
    sums = np.zeros((32, 64))
    for o in range(27):
        sums[o] = stencil[:, 26 - o, :].sum(0)
    sums_stack = np.concatenate(split_np(sums), 0)
    rows = 2 * n_col
    ymatrix = 2.5 * np.eye(rows) - np.eye(rows, k=1) - np.eye(rows, k=-1)
    inverse = np.linalg.inv(ymatrix)
    weights = np.zeros((n_col, n_col, 8, 128), np.float32)
    for own in range(n_col):
        for src in range(n_col):
            for dc in range(3):
                c = src + dc - 1
                if not 0 <= c < n_col:
                    continue
                for lane in range(128):
                    k = lane % 64
                    if k >= 48:
                        continue
                    y = k // 4 % 2
                    y_src = y if lane < 64 else 1 - y
                    weights[own, src, dc, lane] = inverse[2 * own + y, 2 * c + y_src]
    return stack, sums_stack, weights, float(np.float32(stencil[0, 13, 0]))


def split(x):
    high = x.astype(BF16)
    return high, (x - high.astype(F32)).astype(BF16)


def lanes(x, index):
    return jnp.take_along_axis(x, index, axis=1, mode="promise_in_bounds")


def own_sources(v, dx, dy):
    if dx == 1:
        span = range(v, v + 3)
    elif dx == -1:
        span = range(v - 2, v + 1)
    elif dy == 1:
        span = range(v, v + 2)
    elif dy == -1:
        span = range(v - 1, v + 1)
    else:
        span = range(v - 1, v + 2)
    return [w for w in span if 0 <= w < 4]


def kernel(
    n_slab, n_col, centre,
    rhs_hbm, start_hbm, screen_hbm, nbr_hbm, colsend_hbm, slabsend_hbm, cells_hbm, coupling_ref, scale_ref,
    stack_hbm, sums_hbm, weights_hbm,
    out_ref,
    rhs, screen, step, nbr, colsend, slabsend, cells, stack, sums, weights,
    gath, fc, fs, rc, rs_raw, diag, rs, info_s, info_c, in_s, in_c, in_d,
    codes, line_own, line_all, line_w, mix_all, mix_own, row_own, row_all,
    load_sem, send_sem, halo_sem, info_sem, line_sem, mix_sem, row_sem,
):
    s = lax.axis_index("slab")
    c = lax.axis_index("col")
    s_up, s_dn = lax.rem(s + 1, n_slab), lax.rem(s + n_slab - 1, n_slab)
    c_up, c_dn = lax.rem(c + 1, n_col), lax.rem(c + n_col - 1, n_col)

    loads = [
        pltpu.make_async_copy(a, b, load_sem.at[k])
        for k, (a, b) in enumerate([
            (start_hbm, gath.at[pl.ds(0, 64)]),
            (colsend_hbm, colsend),
            (slabsend_hbm, slabsend),
            (cells_hbm, cells),
            (nbr_hbm, nbr),
            (screen_hbm, screen),
            (rhs_hbm, rhs),
            (stack_hbm, stack),
            (sums_hbm, sums),
            (weights_hbm.at[c], weights),
        ])
    ]
    for load in loads:
        load.start()

    barrier = pltpu.get_barrier_semaphore()

    def hello(device):
        pl.semaphore_signal(barrier, inc=1, device_id=device, device_id_type=MESH)

    for device in ((s_up, c_up), (s_up, c_dn), (s_dn, c_up), (s_dn, c_dn)):
        hello(device)

    @pl.loop(1, n_col)
    def _(d):
        hello((s, lax.rem(c + d, n_col)))

    @pl.loop(1, n_slab)
    def _(d):
        hello((lax.rem(s + d, n_slab), c))

    sub = lax.broadcasted_iota(I32, (8, 128), 0)
    lane = lax.broadcasted_iota(I32, (8, 128), 1)
    e_low = lax.rem(sub, 4) < 2

    line_row = jnp.zeros((8, 128), F32)
    for k in range(16):
        line_row = jnp.where(lane == k, coupling_ref[k // 8, k // 4 % 2, k % 4], line_row)
        line_row = jnp.where(lane == 16 + k, scale_ref[k // 8, k // 4 % 2, k % 4], line_row)
    line_own[...] = line_row

    def row8(ref, r, v):
        return jnp.broadcast_to(ref[pl.ds(r, 1), pl.ds(128 * v, 128)], (8, 128))

    for load in loads[:4]:
        load.wait()

    col_index = [row8(colsend, k, 0) for k in range(2)]
    slab_index = [[row8(slabsend, k, v) for v in range(2)] for k in range(2)]

    def pick(index, source, spans, empty):
        low, high = index & 127, index >> 7
        got = jnp.full((8, 128), empty)
        for v in spans:
            got = jnp.where(high == v, lanes(source(v), low), got)
        return got

    def faces(k):
        for a in range(4):
            for bh in range(2):
                t = 2 * a + bh
                source = lambda v: gath[pl.ds(8 * t, 8), pl.ds(128 * v, 128)]
                fc[k, a, bh] = pick(col_index[0 if bh == 0 else 1], source, range(4), 0.0)
                for w in range(2):
                    side = 0 if a < 2 else 1
                    fs[k, a, bh, :, pl.ds(128 * w, 128)] = pick(
                        slab_index[side][w], source, (0,) if side == 0 else (3,), 0.0
                    )

    faces(0)
    cell_source = lambda v: row8(cells, 0, v)
    for k in range(2):
        info_c[k] = pick(col_index[k], cell_source, range(4), NOWHERE)
        for w in range(2):
            got = pick(slab_index[k][w], cell_source, range(4), NOWHERE)
            info_s[k, :, pl.ds(128 * w, 128)] = jnp.where(sub == 0, slab_index[k][w], got)

    pl.semaphore_wait(barrier, 4 + (n_col - 1) + (n_slab - 1))

    def send(src, dst, sent, recv, device):
        copy = pltpu.make_async_remote_copy(
            src_ref=src, dst_ref=dst, send_sem=sent, recv_sem=recv, device_id=device, device_id_type=MESH
        )
        copy.start()
        return copy

    low2, high2 = pl.ds(0, 2), pl.ds(2, 2)

    def send_faces(k):
        return [
            send(src, dst, send_sem.at[8 * k + m], halo_sem.at[8 * k + m], device)
            for m, (src, dst, device) in enumerate([
                (fs.at[k, low2], rs_raw.at[k, low2], (s_dn, c)),
                (fs.at[k, high2], rs_raw.at[k, high2], (s_up, c)),
                (fc.at[k, low2, 0], diag.at[k, low2, 0], (s_dn, c_dn)),
                (fc.at[k, low2, 1], diag.at[k, low2, 1], (s_dn, c_up)),
                (fc.at[k, high2, 0], diag.at[k, high2, 0], (s_up, c_dn)),
                (fc.at[k, high2, 1], diag.at[k, high2, 1], (s_up, c_up)),
                (fc.at[k, :, 0], rc.at[k, :, 0], (s, c_dn)),
                (fc.at[k, :, 1], rc.at[k, :, 1], (s, c_up)),
            ])
        ]

    def bytes_of(ref, sem):
        return pltpu.make_async_copy(ref, ref, sem)

    copies = [send_faces(0)]
    infos = [
        send(src, dst, send_sem.at[16 + m], info_sem.at[m], device)
        for m, (src, dst, device) in enumerate([
            (info_s.at[0], in_s.at[0], (s_dn, c)),
            (info_s.at[1], in_s.at[1], (s_up, c)),
            (info_c.at[0], in_c.at[0], (s, c_dn)),
            (info_c.at[1], in_c.at[1], (s, c_up)),
            (info_c.at[0], in_d.at[0, 0], (s_dn, c_dn)),
            (info_c.at[1], in_d.at[0, 1], (s_dn, c_up)),
            (info_c.at[0], in_d.at[1, 0], (s_up, c_dn)),
            (info_c.at[1], in_d.at[1, 1], (s_up, c_up)),
        ])
    ]
    line_all[pl.ds(s, 1)] = line_own[pl.ds(0, 1)].reshape(1, 1, 128)

    @pl.loop(1, n_slab)
    def _(d):
        send(line_own.at[pl.ds(0, 1)], line_all.at[s], send_sem.at[24], line_sem, (lax.rem(s + d, n_slab), c))

    for load in loads[4:]:
        load.wait()

    def wait_halo(k):
        for copy in copies[k]:
            copy.wait_recv()

    none = -99
    code_cl = jnp.where(c > 0, 0, none)
    code_ch = jnp.where(c < n_col - 1, 1, none)
    code_sl = [jnp.where(s > 0, w, none) for w in range(2)]
    code_sh = [jnp.where(s < n_slab - 1, w, none) for w in range(2)]

    def pattern(dx, dy, sz, v):
        o = 9 * (dx + 1) + 3 * (dy + 1) + 1
        if sz == 0:
            return row8(nbr, o, v)
        return jnp.where(e_low, row8(nbr, o + 1, v), row8(nbr, o - 1, v))

    def groups():
        for v in range(4):
            for blk in range(1, 8):
                sx, sy, sz = blk // 4, blk // 2 % 2, blk % 2
                for dx in ((1, -1) if sx else (0,)):
                    for dy in ((1, -1) if sy else (0,)):
                        halves = range(4) if dx == 0 else ((0, 1) if dx == 1 else (2, 3))
                        bhs = (0, 1) if dy == 0 else ((0,) if dy == 1 else (1,))
                        yield v, blk, dx, dy, sz, [2 * a + bh for a in halves for bh in bhs]

    def gather_own():
        for v, blk, dx, dy, sz, rows in groups():
            index = pattern(dx, dy, sz, v)
            low, high = index & 127, index >> 7
            spans = own_sources(v, dx, dy)
            masks = {w: high == w for w in spans}
            for t in rows:
                got = jnp.zeros((8, 128), F32)
                for w in spans:
                    got = jnp.where(masks[w], lanes(gath[pl.ds(8 * t, 8), pl.ds(128 * w, 128)], low), got)
                gath[pl.ds(64 * blk + 8 * t, 8), pl.ds(128 * v, 128)] = got

    def merge_rims(k):
        for a in range(4):
            side = 0 if a < 2 else 1
            for bh in range(2):
                for w in range(2):
                    at = jnp.broadcast_to(in_s[side, pl.ds(0, 1), pl.ds(128 * w, 128)], (8, 128)) - COL0
                    hit = (at >> 7) == (code_ch if bh == 0 else code_cl)
                    rs[pl.ds(16 * a + 8 * bh, 8), pl.ds(128 * w, 128)] = jnp.where(
                        hit, lanes(diag[k, a, bh], at & 127), rs_raw[k, a, bh, :, pl.ds(128 * w, 128)]
                    )

    def gather_rims(k):
        for v, blk, dx, dy, sz, rows in groups():
            along = (dx == 1 and v == 3) or (dx == -1 and v == 0)
            if dy == 0 and not along:
                continue
            index = pattern(dx, dy, sz, v)
            if dy:
                at_c = index - COL0
                low_c = at_c & 127
                hit_c = (at_c >> 7) == (code_ch if dy == 1 else code_cl)
            if along:
                at_s = index - (SLAB_HIGH if dx == 1 else SLAB_LOW)
                low_s = at_s & 127
                hits = [(at_s >> 7) == code for code in (code_sh if dx == 1 else code_sl)]
            for t in rows:
                where = (pl.ds(64 * blk + 8 * t, 8), pl.ds(128 * v, 128))
                got = gath[where]
                if dy:
                    got = jnp.where(hit_c, lanes(rc[k, t // 2, t % 2], low_c), got)
                if along:
                    for w in range(2):
                        got = jnp.where(hits[w], lanes(rs[pl.ds(8 * t, 8), pl.ds(128 * w, 128)], low_s), got)
                gath[where] = got

    def sweep():
        high, low = split(gath[...])
        both = jnp.dot(stack[...], high, preferred_element_type=F32)
        total = both[:64] + both[64:] + jnp.dot(stack[pl.ds(0, 64)], low, preferred_element_type=F32)
        field = gath[pl.ds(0, 64)]
        return field + step[...] * (rhs[...] - total - screen[...] * field)

    step[...] = RELAX / (centre + screen[...])
    gather_own()
    for copy in infos[:2]:
        copy.wait_recv()
    wait_halo(0)
    merge_rims(0)
    gather_rims(0)
    gath[pl.ds(0, 64)] = sweep()
    faces(1)
    copies.append(send_faces(1))
    gather_own()

    for copy in infos[2:]:
        copy.wait_recv()
    own_codes = [row8(cells, 0, v) + 64 for v in range(4)]
    col_codes = [in_c[1] + 48, in_c[0] + 80]
    slab_codes = []
    for side in (1, 0):
        base = 0 if side == 1 else 96
        parts = []
        for w in range(2):
            at = jnp.broadcast_to(in_s[side, pl.ds(0, 1), pl.ds(128 * w, 128)], (8, 128)) - COL0
            part = jnp.broadcast_to(in_s[side, pl.ds(1, 1), pl.ds(128 * w, 128)], (8, 128)) + base + 16
            part = jnp.where((at >> 7) == 0, lanes(in_d[side, 1], at & 127) + base, part)
            part = jnp.where((at >> 7) == 1, lanes(in_d[side, 0], at & 127) + base + 32, part)
            parts.append(part)
        slab_codes.append(parts)
    for r in range(4):
        for v in range(4):
            if r < 3:
                index = nbr[pl.ds(8 * r, 8), pl.ds(128 * v, 128)]
            else:
                index = jnp.full((8, 128), NB)
                for k in range(3):
                    index = jnp.where(sub == k, row8(nbr, 24 + k, v), index)
            low, high = index & 127, index >> 7
            code = jnp.full((8, 128), NOWHERE)
            for w in range(4):
                code = jnp.where(high == w, lanes(own_codes[w], low), code)
            at = index - COL0
            for m in range(2):
                code = jnp.where((at >> 7) == m, lanes(col_codes[m], at & 127), code)
            if (r < 2 and v == 0) or (r >= 2 and v == 3):
                at = index - (SLAB_LOW if r < 2 else SLAB_HIGH)
                for w in range(2):
                    code = jnp.where((at >> 7) == w, lanes(slab_codes[0 if r < 2 else 1][w], at & 127), code)
            codes[pl.ds(8 * r, 8), pl.ds(128 * v, 128)] = code

    bytes_of(line_all.at[pl.ds(0, n_slab - 1)], line_sem).wait()
    all_rows = line_all[...].reshape(n_slab, 128)
    big_lane = lax.broadcasted_iota(I32, (n_slab, 128), 1)
    big_row = lax.broadcasted_iota(I32, (n_slab, 128), 0)
    spot = big_lane & 7
    c0, c1, p0, p1 = [lanes(all_rows, spot + 8 * k) for k in range(4)]
    first = big_lane < 64
    after, here = big_row > s, big_row == s

    def rows_down(x, d, fill):
        return jnp.where(big_row >= d, pltpu.roll(x, d, 0), fill)

    def rows_up(x, d, fill):
        return jnp.where(big_row < n_slab - d, pltpu.roll(x, n_slab - d, 0), fill)

    run = jnp.where(after, c0 * c1, jnp.where(here, jnp.where(first, c0 * c1, c1), 1.0))
    d = 1
    while d < n_slab:
        run = run * rows_down(run, d, 1.0)
        d *= 2
    run = rows_down(run, 1, 1.0)
    w0 = jnp.where(after, run, jnp.where(here & first, 1.0, 0.0))
    w1 = jnp.where(after, run * c0, jnp.where(here, jnp.where(first, c0, 1.0), 0.0))
    u0, u1 = p0 * w0, p1 * w1
    c0_next = rows_up(c0, 1, 0.0)
    tail, factor = u0 + c1 * u1, c1 * c0_next
    d = 1
    while d < n_slab:
        tail = tail + factor * rows_up(tail, d, 0.0)
        factor = factor * rows_up(factor, d, 0.0)
        d *= 2
    second = u1 + c0_next * rows_up(tail, 1, 0.0)
    give = jnp.where((big_lane & 8) == 0, tail, second)
    part = (big_lane & 63) >> 4
    line_w[...] = jnp.where(
        part == 0, rows_down(give, 1, 0.0), jnp.where(part == 1, give, jnp.where(part == 2, rows_up(give, 1, 0.0), 0.0))
    )

    wait_halo(1)
    merge_rims(1)
    gather_rims(1)
    field = sweep()
    gath[pl.ds(0, 64)] = field

    high, low = split(field)
    both = jnp.dot(sums[...], high, preferred_element_type=F32)
    given = both[:32] + both[32:] + jnp.dot(sums[pl.ds(0, 32)], low, preferred_element_type=F32)
    local = jnp.sum(rhs[...] - screen[...] * field, axis=0, keepdims=True)
    row_at = lax.broadcasted_iota(I32, (32, 512), 0)
    given = (jnp.where(row_at == 13, jnp.broadcast_to(local, (32, 512)), 0.0) - given) * (1.0 / 64.0)

    def fold(parts):
        for bit in (4, 2, 1):
            keep = (sub & bit) == 0
            merged = []
            for k in range(bit):
                one, two = parts[k], parts[k + bit]
                stay, go = jnp.where(keep, one, two), jnp.where(keep, two, one)
                if bit == 4:
                    merged.append(stay + pltpu.roll(go, 4, 0))
                else:
                    merged.append(stay + jnp.where(keep, pltpu.roll(go, 8 - bit, 0), pltpu.roll(go, bit, 0)))
            parts = merged
        return parts[0]

    reach = {
        (0, 0): ((0, 1, 2, 3), range(4)),
        (0, -1): ((0, 1, 2), range(4)),
        (0, 1): ((0, 1, 2, 3), range(4)),
        (-1, 0): ((0, 1), (0,)),
        (-1, -1): ((0,), (0,)),
        (-1, 1): ((0, 1), (0,)),
        (1, 0): ((2, 3), (3,)),
        (1, -1): ((2,), (3,)),
        (1, 1): ((3,), (3,)),
    }
    nought = jnp.zeros((8, 128), F32)
    stacked = []
    for dc in (-1, 0, 1):
        plain, swapped = [], []
        for ds in (-1, 0, 1):
            rs_of, vs_of = reach[(ds, dc)]
            base = 48 * (ds + 1) + 16 * (dc + 1)
            for x in range(2):
                parts = []
                for k in range(8):
                    acc = nought
                    for r in rs_of:
                        for v in vs_of:
                            hit = codes[pl.ds(8 * r, 8), pl.ds(128 * v, 128)] == base + 8 * x + k
                            acc = acc + jnp.where(hit, given[8 * r : 8 * r + 8, 128 * v : 128 * v + 128], 0.0)
                    parts.append(acc)
                total = fold(parts)
                plain.append(total)
                swapped.append(pltpu.roll(total, 4, 0))
        stacked += plain + [nought, nought] + swapped + [nought, nought]
    high, low = split(jnp.concatenate(stacked, axis=0))
    ones = jnp.ones((16, 128), BF16)
    across = (((1,), (1,)), ((), ()))
    summed = lax.dot_general(ones, high, across, preferred_element_type=F32) + lax.dot_general(
        ones, low, across, preferred_element_type=F32
    )
    message = jnp.where(
        sub == 0, summed[:8, :128], jnp.where(sub == 1, summed[:8, 128:256], jnp.where(sub == 2, summed[:8, 256:], 0.0))
    )
    mix_own[...] = message
    mix_all[pl.ds(c, 1)] = message.reshape(1, 8, 128)

    @pl.loop(1, n_col)
    def _(d):
        send(mix_own, mix_all.at[c], send_sem.at[25], mix_sem, (s, lax.rem(c + d, n_col)))

    bytes_of(mix_all.at[pl.ds(0, n_col - 1)], mix_sem).wait()
    mixed = jnp.zeros((8, 128), F32)
    for k in range(n_col):
        mixed = mixed + weights[k] * mix_all[k]
    row = jnp.sum(mixed, axis=0, keepdims=True)
    row = row + pltpu.roll(row, 64, 1)
    row_own[...] = row
    row_all[pl.ds(s, 1)] = row.reshape(1, 1, 128)

    @pl.loop(1, n_slab)
    def _(d):
        send(row_own, row_all.at[s], send_sem.at[26], row_sem, (lax.rem(s + d, n_slab), c))

    bytes_of(row_all.at[pl.ds(0, n_slab - 1)], row_sem).wait()
    corr = jnp.sum(line_w[...] * row_all[...].reshape(n_slab, 128), axis=0, keepdims=True)
    corr = corr + pltpu.roll(corr, 128 - 8, 1)
    corr = corr + pltpu.roll(corr, 128 - 16, 1) + pltpu.roll(corr, 128 - 32, 1)
    corr = jnp.broadcast_to(corr, (8, 128))
    for v in range(4):
        cell = row8(cells, 0, v)
        lift = lanes(corr, (cell >> 3) * 64 + (cell & 7))
        for t in range(8):
            at = (pl.ds(8 * t, 8), pl.ds(128 * v, 128))
            out_ref[at] = gath[at] + lift

    for copy in copies[0] + copies[1] + infos:
        copy.wait_send()
    bytes_of(line_all.at[pl.ds(0, n_slab - 1)], send_sem.at[24]).wait()
    bytes_of(mix_all.at[pl.ds(0, n_col - 1)], send_sem.at[25]).wait()
    bytes_of(row_all.at[pl.ds(0, n_slab - 1)], send_sem.at[26]).wait()


def solution(mesh):
    n_slab, n_col = mesh.shape["slab"], mesh.shape["col"]
    stack, sums, weights, centre = tables(n_col)

    def shards(rhs, start, screen, neighbours, col_send, slab_send, coarse_map, coupling, coarse_scale):
        anywhere = pl.BlockSpec(memory_space=pl.ANY)
        scalars = pl.BlockSpec(memory_space=pltpu.SMEM)
        vmem = pltpu.VMEM
        dma = pltpu.SemaphoreType.DMA
        return pl.pallas_call(
            functools.partial(kernel, n_slab, n_col, centre),
            out_shape=jax.ShapeDtypeStruct((64, NB), F32),
            in_specs=[anywhere] * 7 + [scalars] * 2 + [anywhere] * 3,
            out_specs=pl.BlockSpec(memory_space=pltpu.VMEM),
            scratch_shapes=[
                vmem((64, NB), F32),
                vmem((64, NB), F32),
                vmem((64, NB), F32),
                vmem((27, NB), I32),
                vmem((2, FCOL), I32),
                vmem((2, 256), I32),
                vmem((1, NB), I32),
                vmem((128, 512), BF16),
                vmem((64, 64), BF16),
                vmem((n_col, 8, 128), F32),
                vmem((512, NB), F32),
                vmem((2, 4, 2, 8, 128), F32),
                vmem((2, 4, 2, 8, 256), F32),
                vmem((2, 4, 2, 8, 128), F32),
                vmem((2, 4, 2, 8, 256), F32),
                vmem((2, 4, 2, 8, 128), F32),
                vmem((64, 256), F32),
                vmem((2, 8, 256), I32),
                vmem((2, 8, 128), I32),
                vmem((2, 8, 256), I32),
                vmem((2, 8, 128), I32),
                vmem((2, 2, 8, 128), I32),
                vmem((32, NB), I32),
                vmem((8, 128), F32),
                vmem((n_slab, 1, 128), F32),
                vmem((n_slab, 128), F32),
                vmem((n_col, 8, 128), F32),
                vmem((8, 128), F32),
                vmem((1, 128), F32),
                vmem((n_slab, 1, 128), F32),
                dma((10,)),
                dma((27,)),
                dma((16,)),
                dma((8,)),
                dma,
                dma,
                dma,
            ],
            compiler_params=pltpu.CompilerParams(
                collective_id=0, has_side_effects=True, vmem_limit_bytes=32 * 1024 * 1024
            ),
            cost_estimate=pl.CostEstimate(flops=10**8, bytes_accessed=10**6, transcendentals=0),
        )(
            rhs, start, screen, neighbours, col_send, jnp.pad(slab_send, ((0, 0), (0, 256 - FSLAB))),
            coarse_map.reshape(1, NB), coupling, coarse_scale,
            jnp.asarray(stack), jnp.asarray(sums), jnp.asarray(weights),
        )

    block = P(None, ("slab", "col"))
    line = P("slab", "col", None)
    placed = (block,) * 6 + (P(("slab", "col")), line, line)
    return jax.shard_map(shards, mesh=mesh, in_specs=placed, out_specs=block, check_vma=False)
```

time: 466 us -> 52.6 us (0.11)
  the two profiles are of different devices: /device:TPU:2 before, /device:TPU:1 now
where the time goes in v1:
time: 52.6 us; the launch traced here: 52.2 us
  Pallas kernels  44 us (84%)
  local copies, waits for them, and re-layouts  8.19 us (16%)
    pallas_call x1, Pallas kernels, shards(): pl.pallas_call(functools.partial(kernel, n_slab, n_col, centre), out_shap...  44 us
    unnamed x23, local copies, waits for them, and re-layouts  7.46 us

profile of v1, /device:TPU:1, one launch (start us, length us, event | category | flops | bytes accessed | tf_op | source)
XLA Modules:
  0.0 52.2 jit_solution(4754258808586870430)
XLA Ops:
  0.0 0.0 copy-start.9
  0.0 0.0 copy-start.7
  0.0 0.0 copy-start.8
  0.0 0.7 %pad.4.slabsend_hbm = s32[2,256]{1,0:T(2,128)S(1)} pad(s32[2,160]{1,0:T(2,128)} %param.17, s32[]{:T(128)} %constant.3.clone.1), padding=0_0x0_96 | pad | bytes 3332 | tf_op jit(solution)/shard_map/jit(_pad)/pad | solution.py:585
  0.7 0.0 copy-done.9
  0.7 0.0 copy-done.7
  0.7 0.0 copy-done.8
  0.8 0.0 copy-start
  0.8 0.9 %copy-done = f32[8,8,8,128]{3,2,1,0:T(8,128)S(1)} copy-done((f32[8,8,8,128]{3,2,1,0:T(8,128)S(1)}, f32[8,8,8,128]{3,2,1,0:T(8,128)}, u32[]{:S(2)}) %copy-start) | copy-done | bytes 262168
  1.7 0.0 copy-start.1
  1.7 0.9 %copy-done.1 = f32[64,512]{1,0:T(8,128)S(1)} copy-done((f32[64,512]{1,0:T(8,128)S(1)}, f32[64,512]{1,0:T(8,128)}, u32[]{:S(2)}) %copy-start.1) | copy-done | bytes 131096
  2.6 0.0 copy-start.2
  2.6 0.9 %copy-done.2 = f32[64,512]{1,0:T(8,128)S(1)} copy-done((f32[64,512]{1,0:T(8,128)S(1)}, f32[64,512]{1,0:T(8,128)}, u32[]{:S(2)}) %copy-start.2) | copy-done | bytes 131096
  3.5 0.0 copy-start.3
  3.5 0.9 %copy-done.3 = f32[64,512]{1,0:T(8,128)S(1)} copy-done((f32[64,512]{1,0:T(8,128)S(1)}, f32[64,512]{1,0:T(8,128)}, u32[]{:S(2)}) %copy-start.3) | copy-done | bytes 131096
  4.4 0.0 copy-start.4
  4.4 0.9 %copy-done.4 = bf16[128,512]{1,0:T(8,128)(2,1)S(1)} copy-done((bf16[128,512]{1,0:T(8,128)(2,1)S(1)}, bf16[128,512]{1,0:T(8,128)(2,1)}, u32[]{:S(2)}) %copy-start.4) | copy-done | bytes 131096
  5.3 0.0 copy-start.5
  5.3 0.8 %copy-done.5 = s32[27,512]{1,0:T(8,128)S(1)} copy-done((s32[27,512]{1,0:T(8,128)S(1)}, s32[27,512]{1,0:T(8,128)}, u32[]{:S(2)}) %copy-start.5) | copy-done | bytes 55320
  6.2 0.0 copy-start.6
  6.2 0.7 %copy-done.6 = bf16[64,64]{1,0:T(8,128)(2,1)S(1)} copy-done((bf16[64,64]{1,0:T(8,128)(2,1)S(1)}, bf16[64,64]{1,0:T(8,128)(2,1)}, u32[]{:S(2)}) %copy-start.6) | copy-done | bytes 8216
  6.9 0.0 copy-start.10
  6.9 0.7 %copy-done.10 = s32[2,128]{1,0:T(2,128)S(1)} copy-done((s32[2,128]{1,0:T(2,128)S(1)}, s32[2,128]{1,0:T(2,128)}, u32[]{:S(2)}) %copy-start.10) | copy-done | bytes 1048
  7.6 44.0 %shard_map.118 = f32[64,512]{1,0:T(8,128)S(1)} custom-call(f32[64,512]{1,0:T(8,128)S(1)} %copy-done.1, f32[64,512]{1,0:T(8,128)S(1)} %copy-done.2, f32[64,512]{1,0:T(8,128)S(1)} %copy-done.3, s32[27,512]{1,0:T(8,128)S(1)} %copy-done.5, s32[2,128]{1,0:T(2,128)S(1)} %copy-done.10, s32[2,256]{1,0:T(2,128)S(1)} %pad.4.slabsend_hbm, s32[1,512]{1,0:T(1,128)S(1)} %bitcast.1, ...), custom_call_target="tpu_custom_call" | custom-call | flops 100000000 | bytes 1000000 | tf_op jit(solution)/shard_map/pallas_call | solution.py:536
  51.6 0.7 %copy.14 = f32[64,512]{1,0:T(8,128)} copy(f32[64,512]{1,0:T(8,128)S(1)} %shard_map.118) | data formatting | bytes 262144
Async XLA Ops:
  0.0 0.7 %copy-start.9 = (f32[2,2,4]{2,1,0:T(2,128)S(1)}, f32[2,2,4]{2,1,0:T(2,128)}, u32[]{:S(2)}) copy-start(f32[2,2,4]{2,1,0:T(2,128)} %scale_ref.1) | copy-start | bytes 196
  0.0 0.7 %copy-start.7 = (s32[512]{0:T(512)S(1)}, s32[512]{0:T(512)}, u32[]{:S(2)}) copy-start(s32[512]{0:T(512)} %param.18) | copy-start | bytes 6148
  0.0 0.7 %copy-start.8 = (f32[2,2,4]{2,1,0:T(2,128)S(1)}, f32[2,2,4]{2,1,0:T(2,128)}, u32[]{:S(2)}) copy-start(f32[2,2,4]{2,1,0:T(2,128)} %coupling_ref.1) | copy-start | bytes 196
  0.8 1.0 %copy-start = (f32[8,8,8,128]{3,2,1,0:T(8,128)S(1)}, f32[8,8,8,128]{3,2,1,0:T(8,128)}, u32[]{:S(2)}) copy-start(f32[8,8,8,128]{3,2,1,0:T(8,128)} %constant.10.clone.weights_hbm) | copy-start | bytes 786436
  1.7 0.9 %copy-start.1 = (f32[64,512]{1,0:T(8,128)S(1)}, f32[64,512]{1,0:T(8,128)}, u32[]{:S(2)}) copy-start(f32[64,512]{1,0:T(8,128)} %rhs_hbm.1) | copy-start | bytes 393220
  2.6 0.9 %copy-start.2 = (f32[64,512]{1,0:T(8,128)S(1)}, f32[64,512]{1,0:T(8,128)}, u32[]{:S(2)}) copy-start(f32[64,512]{1,0:T(8,128)} %start_hbm.1) | copy-start | bytes 393220
  3.5 0.9 %copy-start.3 = (f32[64,512]{1,0:T(8,128)S(1)}, f32[64,512]{1,0:T(8,128)}, u32[]{:S(2)}) copy-start(f32[64,512]{1,0:T(8,128)} %screen_hbm.1) | copy-start | bytes 393220
  4.4 0.9 %copy-start.4 = (bf16[128,512]{1,0:T(8,128)(2,1)S(1)}, bf16[128,512]{1,0:T(8,128)(2,1)}, u32[]{:S(2)}) copy-start(bf16[128,512]{1,0:T(8,128)(2,1)} %constant.8.clone.stack_hbm) | copy-start | bytes 393220
  5.3 0.8 %copy-start.5 = (s32[27,512]{1,0:T(8,128)S(1)}, s32[27,512]{1,0:T(8,128)}, u32[]{:S(2)}) copy-start(s32[27,512]{1,0:T(8,128)} %nbr_hbm.1) | copy-start | bytes 165892
  6.2 0.7 %copy-start.6 = (bf16[64,64]{1,0:T(8,128)(2,1)S(1)}, bf16[64,64]{1,0:T(8,128)(2,1)}, u32[]{:S(2)}) copy-start(bf16[64,64]{1,0:T(8,128)(2,1)} %constant.9.clone.sums_hbm) | copy-start | bytes 24580
  6.9 0.7 %copy-start.10 = (s32[2,128]{1,0:T(2,128)S(1)}, s32[2,128]{1,0:T(2,128)}, u32[]{:S(2)}) copy-start(s32[2,128]{1,0:T(2,128)} %colsend_hbm.1) | copy-start | bytes 3076

commit v2 on v1

--- a/solution.py
+++ b/solution.py
@@ -107,10 +107,10 @@
 
 def kernel(
     n_slab, n_col, centre,
-    rhs_hbm, start_hbm, screen_hbm, nbr_hbm, colsend_hbm, slabsend_hbm, cells_hbm, coupling_ref, scale_ref,
+    rhs_hbm, start_hbm, screen_hbm, nbr_hbm, colsend_hbm, slabsend_hbm, cells_hbm, coupling_hbm, scale_hbm,
     stack_hbm, sums_hbm, weights_hbm,
     out_ref,
-    rhs, screen, step, nbr, colsend, slabsend, cells, stack, sums, weights,
+    rhs, screen, step, nbr, colsend, slabsend, cells, coupling_ref, scale_ref, stack, sums, weights,
     gath, fc, fs, rc, rs_raw, diag, rs, info_s, info_c, in_s, in_c, in_d,
     codes, line_own, line_all, line_w, mix_all, mix_own, row_own, row_all,
     load_sem, send_sem, halo_sem, info_sem, line_sem, mix_sem, row_sem,
@@ -127,6 +127,8 @@
             (colsend_hbm, colsend),
             (slabsend_hbm, slabsend),
             (cells_hbm, cells),
+            (coupling_hbm, coupling_ref),
+            (scale_hbm, scale_ref),
             (nbr_hbm, nbr),
             (screen_hbm, screen),
             (rhs_hbm, rhs),
@@ -158,20 +160,27 @@
     lane = lax.broadcasted_iota(I32, (8, 128), 1)
     e_low = lax.rem(sub, 4) < 2
 
+    def row8(ref, r, v):
+        return jnp.broadcast_to(ref[pl.ds(r, 1), pl.ds(128 * v, 128)], (8, 128))
+
+    for load in loads[:6]:
+        load.wait()
+
+    col_index = [row8(colsend, k, 0) for k in range(2)]
+    beyond = jnp.full((1, 256 - FSLAB), NB)
+    slab_index = [
+        [
+            row8(slabsend, k, 0),
+            jnp.broadcast_to(jnp.concatenate([slabsend[pl.ds(k, 1), pl.ds(128, FSLAB - 128)], beyond], axis=1), (8, 128)),
+        ]
+        for k in range(2)
+    ]
+
     line_row = jnp.zeros((8, 128), F32)
     for k in range(16):
         line_row = jnp.where(lane == k, coupling_ref[k // 8, k // 4 % 2, k % 4], line_row)
         line_row = jnp.where(lane == 16 + k, scale_ref[k // 8, k // 4 % 2, k % 4], line_row)
     line_own[...] = line_row
-
-    def row8(ref, r, v):
-        return jnp.broadcast_to(ref[pl.ds(r, 1), pl.ds(128 * v, 128)], (8, 128))
-
-    for load in loads[:4]:
-        load.wait()
-
-    col_index = [row8(colsend, k, 0) for k in range(2)]
-    slab_index = [[row8(slabsend, k, v) for v in range(2)] for k in range(2)]
 
     def pick(index, source, spans, empty):
         low, high = index & 127, index >> 7
@@ -249,7 +258,7 @@
     def _(d):
         send(line_own.at[pl.ds(0, 1)], line_all.at[s], send_sem.at[24], line_sem, (lax.rem(s + d, n_slab), c))
 
-    for load in loads[4:]:
+    for load in loads[6:]:
         load.wait()
 
     def wait_halo(k):
@@ -529,14 +538,13 @@
     stack, sums, weights, centre = tables(n_col)
 
     def shards(rhs, start, screen, neighbours, col_send, slab_send, coarse_map, coupling, coarse_scale):
-        anywhere = pl.BlockSpec(memory_space=pl.ANY)
-        scalars = pl.BlockSpec(memory_space=pltpu.SMEM)
+        hbm = pl.BlockSpec(memory_space=pltpu.HBM)
         vmem = pltpu.VMEM
         dma = pltpu.SemaphoreType.DMA
         return pl.pallas_call(
             functools.partial(kernel, n_slab, n_col, centre),
             out_shape=jax.ShapeDtypeStruct((64, NB), F32),
-            in_specs=[anywhere] * 7 + [scalars] * 2 + [anywhere] * 3,
+            in_specs=[hbm] * 12,
             out_specs=pl.BlockSpec(memory_space=pltpu.VMEM),
             scratch_shapes=[
                 vmem((64, NB), F32),
@@ -544,8 +552,10 @@
                 vmem((64, NB), F32),
                 vmem((27, NB), I32),
                 vmem((2, FCOL), I32),
-                vmem((2, 256), I32),
+                vmem((2, FSLAB), I32),
                 vmem((1, NB), I32),
+                pltpu.SMEM((2, 2, 4), F32),
+                pltpu.SMEM((2, 2, 4), F32),
                 vmem((128, 512), BF16),
                 vmem((64, 64), BF16),
                 vmem((n_col, 8, 128), F32),
@@ -569,7 +579,7 @@
                 vmem((8, 128), F32),
                 vmem((1, 128), F32),
                 vmem((n_slab, 1, 128), F32),
-                dma((10,)),
+                dma((12,)),
                 dma((27,)),
                 dma((16,)),
                 dma((8,)),
@@ -578,11 +588,11 @@
                 dma,
             ],
             compiler_params=pltpu.CompilerParams(
-                collective_id=0, has_side_effects=True, vmem_limit_bytes=32 * 1024 * 1024
+                collective_id=0, has_side_effects=True, vmem_limit_bytes=63 * 1024 * 1024
             ),
             cost_estimate=pl.CostEstimate(flops=10**8, bytes_accessed=10**6, transcendentals=0),
         )(
-            rhs, start, screen, neighbours, col_send, jnp.pad(slab_send, ((0, 0), (0, 256 - FSLAB))),
+            rhs, start, screen, neighbours, col_send, slab_send,
             coarse_map.reshape(1, NB), coupling, coarse_scale,
             jnp.asarray(stack), jnp.asarray(sums), jnp.asarray(weights),
         )

time: 52.6 us -> 44.9 us (0.85)
  local copies, waits for them, and re-layouts: 8.19 us -> 1.57 us
  Pallas kernels: 44 us -> 43.2 us
    unnamed x23 -> x1, local copies, waits for them, and re-layouts: 7.46 us -> 1.57 us
    pallas_call x1, Pallas kernels: 44 us -> 43.2 us  [shards(): pl.pallas_call(functools.partial(kernel, n_slab, n_col, centre), out_shap...]
    pad x1 -> x0, local copies, waits for them, and re-layouts: 0.72 us -> none  [shards(): jnp.pad(slab_send, ((0, 0), (0, 256 - FSLAB)))]
where the time goes in v2:
time: 44.9 us; the launch traced here: 44.8 us
  Pallas kernels  43.2 us (96%)
  local copies, waits for them, and re-layouts  1.57 us (3%)
    pallas_call x1, Pallas kernels, shards(): pl.pallas_call(functools.partial(kernel, n_slab, n_col, centre), out_shap...  43.2 us
    unnamed x1, local copies, waits for them, and re-layouts  1.57 us

profile of v2, /device:TPU:1, one launch (start us, length us, event | category | flops | bytes accessed | tf_op | source)
XLA Modules:
  0.0 44.8 jit_solution(6191133678038449064)
XLA Ops:
  0.0 43.2 %shard_map.118 = f32[64,512]{1,0:T(8,128)} custom-call(f32[64,512]{1,0:T(8,128)} %rhs_hbm.1, f32[64,512]{1,0:T(8,128)} %start_hbm.1, f32[64,512]{1,0:T(8,128)} %screen_hbm.1, s32[27,512]{1,0:T(8,128)} %nbr_hbm.1, s32[2,128]{1,0:T(2,128)} %colsend_hbm.1, s32[2,160]{1,0:T(2,128)} %slabsend_hbm.1, s32[1,512]{1,0:T(1,128)} %bitcast.1, f32[2,2,4]{2,1,0:T(2,128)} %coupling_hbm.1, ...), custom_call_target="tpu_custom_call" | custom-call | flops 100000000 | bytes 1000000 | tf_op jit(solution)/shard_map/pallas_call | solution.py:544
  43.2 1.6 %copy.14 = f32[64,512]{1,0:T(8,128)} copy(f32[64,512]{1,0:T(8,128)} %shard_map.118) | data formatting | bytes 262144

commit v3 on v2

--- a/solution.py
+++ b/solution.py
@@ -113,7 +113,7 @@
     rhs, screen, step, nbr, colsend, slabsend, cells, coupling_ref, scale_ref, stack, sums, weights,
     gath, fc, fs, rc, rs_raw, diag, rs, info_s, info_c, in_s, in_c, in_d,
     codes, line_own, line_all, line_w, mix_all, mix_own, row_own, row_all,
-    load_sem, send_sem, halo_sem, info_sem, line_sem, mix_sem, row_sem,
+    load_sem, send_sem, halo_sem, info_sem, line_sem, mix_sem, row_sem, far_sem,
 ):
     s = lax.axis_index("slab")
     c = lax.axis_index("col")
@@ -152,9 +152,12 @@
     def _(d):
         hello((s, lax.rem(c + d, n_col)))
 
-    @pl.loop(1, n_slab)
+    near = 8 if n_slab >= 32 else 1
+
+    @pl.loop(1, near + 1)
     def _(d):
         hello((lax.rem(s + d, n_slab), c))
+        hello((lax.rem(s + n_slab - d, n_slab), c))
 
     sub = lax.broadcasted_iota(I32, (8, 128), 0)
     lane = lax.broadcasted_iota(I32, (8, 128), 1)
@@ -209,7 +212,25 @@
             got = pick(slab_index[k][w], cell_source, range(4), NOWHERE)
             info_s[k, :, pl.ds(128 * w, 128)] = jnp.where(sub == 0, slab_index[k][w], got)
 
-    pl.semaphore_wait(barrier, 4 + (n_col - 1) + (n_slab - 1))
+    pl.semaphore_wait(barrier, 4 + (n_col - 1) + 2 * near)
+
+    reaches = []
+    while near < n_slab // 2:
+        reaches.append(near)
+        near *= 2
+
+    def tell(k):
+        if k < len(reaches):
+            for d in (reaches[k], n_slab - reaches[k]):
+                pl.semaphore_signal(
+                    far_sem.at[k], inc=1, device_id=(lax.rem(s + d, n_slab), c), device_id_type=MESH
+                )
+
+    def hear(k):
+        if k < len(reaches):
+            pl.semaphore_wait(far_sem.at[k], 2)
+
+    tell(0)
 
     def send(src, dst, sent, recv, device):
         copy = pltpu.make_async_remote_copy(
@@ -252,12 +273,6 @@
             (info_c.at[1], in_d.at[1, 1], (s_up, c_up)),
         ])
     ]
-    line_all[pl.ds(s, 1)] = line_own[pl.ds(0, 1)].reshape(1, 1, 128)
-
-    @pl.loop(1, n_slab)
-    def _(d):
-        send(line_own.at[pl.ds(0, 1)], line_all.at[s], send_sem.at[24], line_sem, (lax.rem(s + d, n_slab), c))
-
     for load in loads[6:]:
         load.wait()
 
@@ -346,6 +361,8 @@
     for copy in infos[:2]:
         copy.wait_recv()
     wait_halo(0)
+    hear(0)
+    tell(1)
     merge_rims(0)
     gather_rims(0)
     gath[pl.ds(0, 64)] = sweep()
@@ -389,45 +406,8 @@
                     code = jnp.where((at >> 7) == w, lanes(slab_codes[0 if r < 2 else 1][w], at & 127), code)
             codes[pl.ds(8 * r, 8), pl.ds(128 * v, 128)] = code
 
-    bytes_of(line_all.at[pl.ds(0, n_slab - 1)], line_sem).wait()
-    all_rows = line_all[...].reshape(n_slab, 128)
-    big_lane = lax.broadcasted_iota(I32, (n_slab, 128), 1)
-    big_row = lax.broadcasted_iota(I32, (n_slab, 128), 0)
-    spot = big_lane & 7
-    c0, c1, p0, p1 = [lanes(all_rows, spot + 8 * k) for k in range(4)]
-    first = big_lane < 64
-    after, here = big_row > s, big_row == s
-
-    def rows_down(x, d, fill):
-        return jnp.where(big_row >= d, pltpu.roll(x, d, 0), fill)
-
-    def rows_up(x, d, fill):
-        return jnp.where(big_row < n_slab - d, pltpu.roll(x, n_slab - d, 0), fill)
-
-    run = jnp.where(after, c0 * c1, jnp.where(here, jnp.where(first, c0 * c1, c1), 1.0))
-    d = 1
-    while d < n_slab:
-        run = run * rows_down(run, d, 1.0)
-        d *= 2
-    run = rows_down(run, 1, 1.0)
-    w0 = jnp.where(after, run, jnp.where(here & first, 1.0, 0.0))
-    w1 = jnp.where(after, run * c0, jnp.where(here, jnp.where(first, c0, 1.0), 0.0))
-    u0, u1 = p0 * w0, p1 * w1
-    c0_next = rows_up(c0, 1, 0.0)
-    tail, factor = u0 + c1 * u1, c1 * c0_next
-    d = 1
-    while d < n_slab:
-        tail = tail + factor * rows_up(tail, d, 0.0)
-        factor = factor * rows_up(factor, d, 0.0)
-        d *= 2
-    second = u1 + c0_next * rows_up(tail, 1, 0.0)
-    give = jnp.where((big_lane & 8) == 0, tail, second)
-    part = (big_lane & 63) >> 4
-    line_w[...] = jnp.where(
-        part == 0, rows_down(give, 1, 0.0), jnp.where(part == 1, give, jnp.where(part == 2, rows_up(give, 1, 0.0), 0.0))
-    )
-
     wait_halo(1)
+    hear(1)
     merge_rims(1)
     gather_rims(1)
     field = sweep()
@@ -501,6 +481,12 @@
     def _(d):
         send(mix_own, mix_all.at[c], send_sem.at[25], mix_sem, (s, lax.rem(c + d, n_col)))
 
+    line_all[pl.ds(s, 1)] = line_own[pl.ds(0, 1)].reshape(1, 1, 128)
+
+    @pl.loop(1, n_slab)
+    def _(d):
+        send(line_own.at[pl.ds(0, 1)], line_all.at[s], send_sem.at[24], line_sem, (lax.rem(s + d, n_slab), c))
+
     bytes_of(mix_all.at[pl.ds(0, n_col - 1)], mix_sem).wait()
     mixed = jnp.zeros((8, 128), F32)
     for k in range(n_col):
@@ -513,6 +499,44 @@
     @pl.loop(1, n_slab)
     def _(d):
         send(row_own, row_all.at[s], send_sem.at[26], row_sem, (lax.rem(s + d, n_slab), c))
+
+    bytes_of(line_all.at[pl.ds(0, n_slab - 1)], line_sem).wait()
+    all_rows = line_all[...].reshape(n_slab, 128)
+    big_lane = lax.broadcasted_iota(I32, (n_slab, 128), 1)
+    big_row = lax.broadcasted_iota(I32, (n_slab, 128), 0)
+    spot = big_lane & 7
+    c0, c1, p0, p1 = [lanes(all_rows, spot + 8 * k) for k in range(4)]
+    first = big_lane < 64
+    after, here = big_row > s, big_row == s
+
+    def rows_down(x, d, fill):
+        return jnp.where(big_row >= d, pltpu.roll(x, d, 0), fill)
+
+    def rows_up(x, d, fill):
+        return jnp.where(big_row < n_slab - d, pltpu.roll(x, n_slab - d, 0), fill)
+
+    run = jnp.where(after, c0 * c1, jnp.where(here, jnp.where(first, c0 * c1, c1), 1.0))
+    d = 1
+    while d < n_slab:
+        run = run * rows_down(run, d, 1.0)
+        d *= 2
+    run = rows_down(run, 1, 1.0)
+    w0 = jnp.where(after, run, jnp.where(here & first, 1.0, 0.0))
+    w1 = jnp.where(after, run * c0, jnp.where(here, jnp.where(first, c0, 1.0), 0.0))
+    u0, u1 = p0 * w0, p1 * w1
+    c0_next = rows_up(c0, 1, 0.0)
+    tail, factor = u0 + c1 * u1, c1 * c0_next
+    d = 1
+    while d < n_slab:
+        tail = tail + factor * rows_up(tail, d, 0.0)
+        factor = factor * rows_up(factor, d, 0.0)
+        d *= 2
+    second = u1 + c0_next * rows_up(tail, 1, 0.0)
+    give = jnp.where((big_lane & 8) == 0, tail, second)
+    part = (big_lane & 63) >> 4
+    line_w[...] = jnp.where(
+        part == 0, rows_down(give, 1, 0.0), jnp.where(part == 1, give, jnp.where(part == 2, rows_up(give, 1, 0.0), 0.0))
+    )
 
     bytes_of(row_all.at[pl.ds(0, n_slab - 1)], row_sem).wait()
     corr = jnp.sum(line_w[...] * row_all[...].reshape(n_slab, 128), axis=0, keepdims=True)
@@ -586,6 +610,7 @@
                 dma,
                 dma,
                 dma,
+                pltpu.SemaphoreType.REGULAR((2,)),
             ],
             compiler_params=pltpu.CompilerParams(
                 collective_id=0, has_side_effects=True, vmem_limit_bytes=63 * 1024 * 1024

time: 44.9 us -> 41.6 us (0.927)
  Pallas kernels: 43.2 us -> 39.9 us
    pallas_call x1, Pallas kernels: 43.2 us -> 39.9 us  [shards(): pl.pallas_call(functools.partial(kernel, n_slab, n_col, centre), out_shap...]
where the time goes in v3:
time: 41.6 us; the launch traced here: 41.5 us
  Pallas kernels  39.9 us (96%)
  local copies, waits for them, and re-layouts  1.57 us (4%)
    pallas_call x1, Pallas kernels, shards(): pl.pallas_call(functools.partial(kernel, n_slab, n_col, centre), out_shap...  39.9 us
    unnamed x1, local copies, waits for them, and re-layouts  1.57 us

profile of v3, /device:TPU:1, one launch (start us, length us, event | category | flops | bytes accessed | tf_op | source)
XLA Modules:
  0.0 41.5 jit_solution(11169386541327932922)
XLA Ops:
  0.0 39.9 %shard_map.118 = f32[64,512]{1,0:T(8,128)} custom-call(f32[64,512]{1,0:T(8,128)} %rhs_hbm.1, f32[64,512]{1,0:T(8,128)} %start_hbm.1, f32[64,512]{1,0:T(8,128)} %screen_hbm.1, s32[27,512]{1,0:T(8,128)} %nbr_hbm.1, s32[2,128]{1,0:T(2,128)} %colsend_hbm.1, s32[2,160]{1,0:T(2,128)} %slabsend_hbm.1, s32[1,512]{1,0:T(1,128)} %bitcast.1, f32[2,2,4]{2,1,0:T(2,128)} %coupling_hbm.1, ...), custom_call_target="tpu_custom_call" | custom-call | flops 100000000 | bytes 1000000 | tf_op jit(solution)/shard_map/pallas_call | solution.py:568
  39.9 1.6 %copy.14 = f32[64,512]{1,0:T(8,128)} copy(f32[64,512]{1,0:T(8,128)} %shard_map.118) | data formatting | bytes 262144

commit v4 on v3

--- a/solution.py
+++ b/solution.py
@@ -19,6 +19,8 @@
 COL0 = NB + 1
 SLAB_LOW = COL0 + 2 * FCOL
 SLAB_HIGH = SLAB_LOW + FSLAB
+AT_CL, AT_CH, AT_SLAB, AT_DL, AT_DH, AT_NONE = 5, 6, 10, 11, 12, 13
+BLOCKS = (0, 1, 4, 5, 2, 3, 6, 7)
 NOWHERE = -1000
 
 
@@ -49,14 +51,14 @@
 def tables(n_col):
     stencil = stencil_table()
     packed = np.zeros((64, 512))
-    for blk in range(8):
+    for at, blk in enumerate(BLOCKS):
         sx, sy, sz = blk // 4, blk // 2 % 2, blk % 2
         for j in range(64):
             a, b, e = j // 16, j // 4 % 4, j % 4
             dx = sx * (1 if a < 2 else -1)
             dy = sy * (1 if b < 2 else -1)
             dz = sz * (1 if e < 2 else -1)
-            packed[:, blk * 64 + j] = stencil[:, 9 * (dx + 1) + 3 * (dy + 1) + dz + 1, j]
+            packed[:, at * 64 + j] = stencil[:, 9 * (dx + 1) + 3 * (dy + 1) + dz + 1, j]
     stack = np.concatenate(split_np(packed), 0)
     sums = np.zeros((32, 64))
     for o in range(27):
@@ -109,16 +111,30 @@
     n_slab, n_col, centre,
     rhs_hbm, start_hbm, screen_hbm, nbr_hbm, colsend_hbm, slabsend_hbm, cells_hbm, coupling_hbm, scale_hbm,
     stack_hbm, sums_hbm, weights_hbm,
-    out_ref,
+    out_hbm,
     rhs, screen, step, nbr, colsend, slabsend, cells, coupling_ref, scale_ref, stack, sums, weights,
-    gath, fc, fs, rc, rs_raw, diag, rs, info_s, info_c, in_s, in_c, in_d,
+    gath, edge, base, nbn, fc, fs, rc, rs, diag, info_s, info_c, in_s, in_c, in_d,
     codes, line_own, line_all, line_w, mix_all, mix_own, row_own, row_all,
-    load_sem, send_sem, halo_sem, info_sem, line_sem, mix_sem, row_sem, far_sem,
+    load_sem, out_sem, send_sem, halo_sem, info_sem, line_sem, mix_sem, row_sem, far_sem,
 ):
     s = lax.axis_index("slab")
     c = lax.axis_index("col")
     s_up, s_dn = lax.rem(s + 1, n_slab), lax.rem(s + n_slab - 1, n_slab)
     c_up, c_dn = lax.rem(c + 1, n_col), lax.rem(c + n_col - 1, n_col)
+
+    barrier = pltpu.get_barrier_semaphore()
+
+    def hello(device):
+        pl.semaphore_signal(barrier, inc=1, device_id=device, device_id_type=MESH)
+
+    near = 4 if n_slab >= 32 else 1
+    for device in ((s_up, c_up), (s_up, c_dn), (s_dn, c_up), (s_dn, c_dn)):
+        hello(device)
+    for d in range(1, near + 1):
+        hello((lax.rem(s + d, n_slab), c))
+        hello((lax.rem(s + n_slab - d, n_slab), c))
+    hello((s, c_up))
+    hello((s, c_dn))
 
     loads = [
         pltpu.make_async_copy(a, b, load_sem.at[k])
@@ -140,25 +156,6 @@
     for load in loads:
         load.start()
 
-    barrier = pltpu.get_barrier_semaphore()
-
-    def hello(device):
-        pl.semaphore_signal(barrier, inc=1, device_id=device, device_id_type=MESH)
-
-    for device in ((s_up, c_up), (s_up, c_dn), (s_dn, c_up), (s_dn, c_dn)):
-        hello(device)
-
-    @pl.loop(1, n_col)
-    def _(d):
-        hello((s, lax.rem(c + d, n_col)))
-
-    near = 8 if n_slab >= 32 else 1
-
-    @pl.loop(1, near + 1)
-    def _(d):
-        hello((lax.rem(s + d, n_slab), c))
-        hello((lax.rem(s + n_slab - d, n_slab), c))
-
     sub = lax.broadcasted_iota(I32, (8, 128), 0)
     lane = lax.broadcasted_iota(I32, (8, 128), 1)
     e_low = lax.rem(sub, 4) < 2
@@ -197,22 +194,17 @@
             for bh in range(2):
                 t = 2 * a + bh
                 source = lambda v: gath[pl.ds(8 * t, 8), pl.ds(128 * v, 128)]
+                fs[k, a, bh] = source(0 if a < 2 else 3)
                 fc[k, a, bh] = pick(col_index[0 if bh == 0 else 1], source, range(4), 0.0)
-                for w in range(2):
-                    side = 0 if a < 2 else 1
-                    fs[k, a, bh, :, pl.ds(128 * w, 128)] = pick(
-                        slab_index[side][w], source, (0,) if side == 0 else (3,), 0.0
-                    )
 
     faces(0)
     cell_source = lambda v: row8(cells, 0, v)
     for k in range(2):
         info_c[k] = pick(col_index[k], cell_source, range(4), NOWHERE)
         for w in range(2):
-            got = pick(slab_index[k][w], cell_source, range(4), NOWHERE)
-            info_s[k, :, pl.ds(128 * w, 128)] = jnp.where(sub == 0, slab_index[k][w], got)
-
-    pl.semaphore_wait(barrier, 4 + (n_col - 1) + 2 * near)
+            info_s[k, :, pl.ds(128 * w, 128)] = jnp.where(sub == 0, slab_index[k][w], cell_source(3 * k))
+
+    pl.semaphore_wait(barrier, 6 + 2 * near)
 
     reaches = []
     while near < n_slab // 2:
@@ -230,6 +222,8 @@
         if k < len(reaches):
             pl.semaphore_wait(far_sem.at[k], 2)
 
+    across_far = n_col > 4
+
     tell(0)
 
     def send(src, dst, sent, recv, device):
@@ -245,12 +239,12 @@
         return [
             send(src, dst, send_sem.at[8 * k + m], halo_sem.at[8 * k + m], device)
             for m, (src, dst, device) in enumerate([
-                (fs.at[k, low2], rs_raw.at[k, low2], (s_dn, c)),
-                (fs.at[k, high2], rs_raw.at[k, high2], (s_up, c)),
                 (fc.at[k, low2, 0], diag.at[k, low2, 0], (s_dn, c_dn)),
                 (fc.at[k, low2, 1], diag.at[k, low2, 1], (s_dn, c_up)),
                 (fc.at[k, high2, 0], diag.at[k, high2, 0], (s_up, c_dn)),
                 (fc.at[k, high2, 1], diag.at[k, high2, 1], (s_up, c_up)),
+                (fs.at[k, low2], rs.at[k, low2], (s_dn, c)),
+                (fs.at[k, high2], rs.at[k, high2], (s_up, c)),
                 (fc.at[k, :, 0], rc.at[k, :, 0], (s, c_dn)),
                 (fc.at[k, :, 1], rc.at[k, :, 1], (s, c_up)),
             ])
@@ -280,138 +274,155 @@
         for copy in copies[k]:
             copy.wait_recv()
 
-    none = -99
-    code_cl = jnp.where(c > 0, 0, none)
-    code_ch = jnp.where(c < n_col - 1, 1, none)
-    code_sl = [jnp.where(s > 0, w, none) for w in range(2)]
-    code_sh = [jnp.where(s < n_slab - 1, w, none) for w in range(2)]
+    def place(there, at):
+        return 128 * jnp.where(there, at, AT_NONE)
+
+    above, below, right, left = s < n_slab - 1, s > 0, c < n_col - 1, c > 0
+
+    def raw_rows(r, v):
+        if r < 3:
+            return nbr[pl.ds(8 * r, 8), pl.ds(128 * v, 128)]
+        index = jnp.full((8, 128), NB)
+        for k in range(3):
+            index = jnp.where(sub == k, row8(nbr, 24 + k, v), index)
+        return index
+
+    def place_col(index):
+        at = index - COL0
+        got = jnp.where(index < NB, index, 128 * AT_NONE)
+        got = jnp.where((at >> 7) == 0, place(left, AT_CL) + (at & 127), got)
+        return jnp.where((at >> 7) == 1, place(right, AT_CH) + (at & 127), got)
+
+    def place_slab(index, got, up):
+        at = index - (SLAB_HIGH if up else SLAB_LOW)
+        side, there = (0, above) if up else (1, below)
+        listed = jnp.full((8, 128), NB)
+        for w in range(2):
+            table = jnp.broadcast_to(in_s[side, pl.ds(0, 1), pl.ds(128 * w, 128)], (8, 128))
+            listed = jnp.where((at >> 7) == w, lanes(table, at & 127), listed)
+        col = listed - COL0
+        spot = jnp.where((listed >> 7) == (0 if up else 3), place(there, AT_SLAB) + (listed & 127), 128 * AT_NONE)
+        spot = jnp.where((col >> 7) == 0, place(there & left, AT_DL) + (col & 127), spot)
+        spot = jnp.where((col >> 7) == 1, place(there & right, AT_DH) + (col & 127), spot)
+        return jnp.where((at >= 0) & (at < FSLAB), spot, got)
 
     def pattern(dx, dy, sz, v):
         o = 9 * (dx + 1) + 3 * (dy + 1) + 1
         if sz == 0:
-            return row8(nbr, o, v)
-        return jnp.where(e_low, row8(nbr, o + 1, v), row8(nbr, o - 1, v))
-
-    def groups():
+            return row8(nbn, o, v)
+        return jnp.where(e_low, row8(nbn, o + 1, v), row8(nbn, o - 1, v))
+
+    def groups(v):
+        for at, blk in enumerate(BLOCKS):
+            if blk == 0:
+                continue
+            sx, sy, sz = blk // 4, blk // 2 % 2, blk % 2
+            for dx in ((1, -1) if sx else (0,)):
+                for dy in ((1, -1) if sy else (0,)):
+                    halves = range(4) if dx == 0 else ((0, 1) if dx == 1 else (2, 3))
+                    bhs = (0, 1) if dy == 0 else ((0,) if dy == 1 else (1,))
+                    yield at, dx, dy, sz, [2 * a + bh for a in halves for bh in bhs]
+
+    def gather_own():
         for v in range(4):
-            for blk in range(1, 8):
-                sx, sy, sz = blk // 4, blk // 2 % 2, blk % 2
-                for dx in ((1, -1) if sx else (0,)):
-                    for dy in ((1, -1) if sy else (0,)):
-                        halves = range(4) if dx == 0 else ((0, 1) if dx == 1 else (2, 3))
-                        bhs = (0, 1) if dy == 0 else ((0,) if dy == 1 else (1,))
-                        yield v, blk, dx, dy, sz, [2 * a + bh for a in halves for bh in bhs]
-
-    def gather_own():
-        for v, blk, dx, dy, sz, rows in groups():
-            index = pattern(dx, dy, sz, v)
-            low, high = index & 127, index >> 7
-            spans = own_sources(v, dx, dy)
-            masks = {w: high == w for w in spans}
-            for t in rows:
-                got = jnp.zeros((8, 128), F32)
-                for w in spans:
-                    got = jnp.where(masks[w], lanes(gath[pl.ds(8 * t, 8), pl.ds(128 * w, 128)], low), got)
-                gath[pl.ds(64 * blk + 8 * t, 8), pl.ds(128 * v, 128)] = got
-
-    def merge_rims(k):
-        for a in range(4):
-            side = 0 if a < 2 else 1
-            for bh in range(2):
-                for w in range(2):
-                    at = jnp.broadcast_to(in_s[side, pl.ds(0, 1), pl.ds(128 * w, 128)], (8, 128)) - COL0
-                    hit = (at >> 7) == (code_ch if bh == 0 else code_cl)
-                    rs[pl.ds(16 * a + 8 * bh, 8), pl.ds(128 * w, 128)] = jnp.where(
-                        hit, lanes(diag[k, a, bh], at & 127), rs_raw[k, a, bh, :, pl.ds(128 * w, 128)]
-                    )
-
-    def gather_rims(k):
-        for v, blk, dx, dy, sz, rows in groups():
+            for blk, dx, dy, sz, rows in groups(v):
+                index = pattern(dx, dy, sz, v)
+                low, high = index & 127, index >> 7
+                spans = own_sources(v, dx, dy)
+                masks = {w: high == w for w in spans}
+                for t in rows:
+                    got = jnp.zeros((8, 128), F32)
+                    for w in spans:
+                        got = jnp.where(masks[w], lanes(gath[pl.ds(8 * t, 8), pl.ds(128 * w, 128)], low), got)
+                    gath[pl.ds(64 * blk + 8 * t, 8), pl.ds(128 * v, 128)] = got
+
+    def gather_rims(k, v, slot, half):
+        for blk, dx, dy, sz, rows in groups(v):
             along = (dx == 1 and v == 3) or (dx == -1 and v == 0)
             if dy == 0 and not along:
                 continue
             index = pattern(dx, dy, sz, v)
-            if dy:
-                at_c = index - COL0
-                low_c = at_c & 127
-                hit_c = (at_c >> 7) == (code_ch if dy == 1 else code_cl)
-            if along:
-                at_s = index - (SLAB_HIGH if dx == 1 else SLAB_LOW)
-                low_s = at_s & 127
-                hits = [(at_s >> 7) == code for code in (code_sh if dx == 1 else code_sl)]
+            low, high = index & 127, index >> 7
             for t in rows:
-                where = (pl.ds(64 * blk + 8 * t, 8), pl.ds(128 * v, 128))
-                got = gath[where]
+                a, bh = t // 2, t % 2
+                got = jnp.zeros((8, 128), F32)
                 if dy:
-                    got = jnp.where(hit_c, lanes(rc[k, t // 2, t % 2], low_c), got)
+                    got = jnp.where(high == (AT_CH if dy == 1 else AT_CL), lanes(rc[k, a, bh], low), got)
                 if along:
-                    for w in range(2):
-                        got = jnp.where(hits[w], lanes(rs[pl.ds(8 * t, 8), pl.ds(128 * w, 128)], low_s), got)
-                gath[where] = got
-
-    def sweep():
-        high, low = split(gath[...])
-        both = jnp.dot(stack[...], high, preferred_element_type=F32)
-        total = both[:64] + both[64:] + jnp.dot(stack[pl.ds(0, 64)], low, preferred_element_type=F32)
+                    got = jnp.where(high == AT_SLAB, lanes(rs[k, a, bh], low), got)
+                    if dy:
+                        got = jnp.where(high == (AT_DH if dy == 1 else AT_DL), lanes(diag[k, a, bh], low), got)
+                edge[half, pl.ds(64 * (blk - 2) + 8 * t, 8), pl.ds(128 * slot, 128)] = got
+
+    def product(source, rows):
+        high, low = split(source)
+        both = jnp.dot(stack[:, rows], high, preferred_element_type=F32)
+        return both[:64] + both[64:] + jnp.dot(stack[pl.ds(0, 64), rows], low, preferred_element_type=F32)
+
+    def sweep_own():
+        gather_own()
         field = gath[pl.ds(0, 64)]
-        return field + step[...] * (rhs[...] - total - screen[...] * field)
+        total = product(gath[...], pl.ds(0, 512))
+        base[...] = field + step[...] * (rhs[...] - total - screen[...] * field)
+
+    def sweep_rims(k):
+        for half, vs in ((0, (1, 2)), (1, (0, 3))):
+            for slot, v in enumerate(vs):
+                gather_rims(k, v, slot, half)
+            first = 256 if half == 0 else 128
+            total = product(edge[half, pl.ds(first - 128, 512 - first)], pl.ds(first, 512 - first))
+            for slot, v in enumerate(vs):
+                at = pl.ds(128 * v, 128)
+                gath[pl.ds(0, 64), at] = base[:, at] - step[:, at] * total[:, 128 * slot : 128 * slot + 128]
 
     step[...] = RELAX / (centre + screen[...])
-    gather_own()
+    edge[1, pl.ds(0, 128)] = jnp.zeros((128, 256), F32)
+    for r in range(4):
+        for v in range(4):
+            nbn[pl.ds(8 * r, 8), pl.ds(128 * v, 128)] = place_col(raw_rows(r, v))
+    sweep_own()
     for copy in infos[:2]:
         copy.wait_recv()
+    for r in range(4):
+        at = (pl.ds(8 * r, 8), pl.ds(0 if r < 2 else 384, 128))
+        nbn[at] = place_slab(raw_rows(r, 0 if r < 2 else 3), nbn[at], r >= 2)
     wait_halo(0)
     hear(0)
     tell(1)
-    merge_rims(0)
-    gather_rims(0)
-    gath[pl.ds(0, 64)] = sweep()
+    if across_far:
+        for d in (2, n_col - 2):
+            pl.semaphore_signal(far_sem.at[3], inc=1, device_id=(s, lax.rem(c + d, n_col)), device_id_type=MESH)
+    sweep_rims(0)
     faces(1)
     copies.append(send_faces(1))
-    gather_own()
+    sweep_own()
 
     for copy in infos[2:]:
         copy.wait_recv()
     own_codes = [row8(cells, 0, v) + 64 for v in range(4)]
     col_codes = [in_c[1] + 48, in_c[0] + 80]
-    slab_codes = []
-    for side in (1, 0):
-        base = 0 if side == 1 else 96
-        parts = []
-        for w in range(2):
-            at = jnp.broadcast_to(in_s[side, pl.ds(0, 1), pl.ds(128 * w, 128)], (8, 128)) - COL0
-            part = jnp.broadcast_to(in_s[side, pl.ds(1, 1), pl.ds(128 * w, 128)], (8, 128)) + base + 16
-            part = jnp.where((at >> 7) == 0, lanes(in_d[side, 1], at & 127) + base, part)
-            part = jnp.where((at >> 7) == 1, lanes(in_d[side, 0], at & 127) + base + 32, part)
-            parts.append(part)
-        slab_codes.append(parts)
     for r in range(4):
         for v in range(4):
-            if r < 3:
-                index = nbr[pl.ds(8 * r, 8), pl.ds(128 * v, 128)]
-            else:
-                index = jnp.full((8, 128), NB)
-                for k in range(3):
-                    index = jnp.where(sub == k, row8(nbr, 24 + k, v), index)
+            index = nbn[pl.ds(8 * r, 8), pl.ds(128 * v, 128)]
             low, high = index & 127, index >> 7
             code = jnp.full((8, 128), NOWHERE)
             for w in range(4):
                 code = jnp.where(high == w, lanes(own_codes[w], low), code)
-            at = index - COL0
-            for m in range(2):
-                code = jnp.where((at >> 7) == m, lanes(col_codes[m], at & 127), code)
+            for w, at in enumerate((AT_CL, AT_CH)):
+                code = jnp.where(high == at, lanes(col_codes[w], low), code)
             if (r < 2 and v == 0) or (r >= 2 and v == 3):
-                at = index - (SLAB_LOW if r < 2 else SLAB_HIGH)
-                for w in range(2):
-                    code = jnp.where((at >> 7) == w, lanes(slab_codes[0 if r < 2 else 1][w], at & 127), code)
+                side, first = (1, 0) if r < 2 else (0, 96)
+                beside = jnp.broadcast_to(in_s[side, pl.ds(1, 1), pl.ds(0, 128)], (8, 128))
+                code = jnp.where(high == AT_SLAB, lanes(beside, low) + first + 16, code)
+                code = jnp.where(high == AT_DL, lanes(in_d[side, 1], low) + first, code)
+                code = jnp.where(high == AT_DH, lanes(in_d[side, 0], low) + first + 32, code)
             codes[pl.ds(8 * r, 8), pl.ds(128 * v, 128)] = code
 
+    hear(1)
+    tell(2)
     wait_halo(1)
-    hear(1)
-    merge_rims(1)
-    gather_rims(1)
-    field = sweep()
-    gath[pl.ds(0, 64)] = field
+    sweep_rims(1)
+    field = gath[pl.ds(0, 64)]
 
     high, low = split(field)
     both = jnp.dot(sums[...], high, preferred_element_type=F32)
@@ -451,14 +462,14 @@
         plain, swapped = [], []
         for ds in (-1, 0, 1):
             rs_of, vs_of = reach[(ds, dc)]
-            base = 48 * (ds + 1) + 16 * (dc + 1)
+            first_code = 48 * (ds + 1) + 16 * (dc + 1)
             for x in range(2):
                 parts = []
                 for k in range(8):
                     acc = nought
                     for r in rs_of:
                         for v in vs_of:
-                            hit = codes[pl.ds(8 * r, 8), pl.ds(128 * v, 128)] == base + 8 * x + k
+                            hit = codes[pl.ds(8 * r, 8), pl.ds(128 * v, 128)] == first_code + 8 * x + k
                             acc = acc + jnp.where(hit, given[8 * r : 8 * r + 8, 128 * v : 128 * v + 128], 0.0)
                     parts.append(acc)
                 total = fold(parts)
@@ -474,6 +485,8 @@
     message = jnp.where(
         sub == 0, summed[:8, :128], jnp.where(sub == 1, summed[:8, 128:256], jnp.where(sub == 2, summed[:8, 256:], 0.0))
     )
+    if across_far:
+        pl.semaphore_wait(far_sem.at[3], 2)
     mix_own[...] = message
     mix_all[pl.ds(c, 1)] = message.reshape(1, 8, 128)
 
@@ -481,6 +494,7 @@
     def _(d):
         send(mix_own, mix_all.at[c], send_sem.at[25], mix_sem, (s, lax.rem(c + d, n_col)))
 
+    hear(2)
     line_all[pl.ds(s, 1)] = line_own[pl.ds(0, 1)].reshape(1, 1, 128)
 
     @pl.loop(1, n_slab)
@@ -496,7 +510,7 @@
     row_own[...] = row
     row_all[pl.ds(s, 1)] = row.reshape(1, 1, 128)
 
-    @pl.loop(1, n_slab)
+    @pl.loop(1, n_slab, unroll=9 if n_slab == 64 else 1)
     def _(d):
         send(row_own, row_all.at[s], send_sem.at[26], row_sem, (lax.rem(s + d, n_slab), c))
 
@@ -543,18 +557,23 @@
     corr = corr + pltpu.roll(corr, 128 - 8, 1)
     corr = corr + pltpu.roll(corr, 128 - 16, 1) + pltpu.roll(corr, 128 - 32, 1)
     corr = jnp.broadcast_to(corr, (8, 128))
+    results = []
     for v in range(4):
         cell = row8(cells, 0, v)
         lift = lanes(corr, (cell >> 3) * 64 + (cell & 7))
+        at = pl.ds(128 * v, 128)
         for t in range(8):
-            at = (pl.ds(8 * t, 8), pl.ds(128 * v, 128))
-            out_ref[at] = gath[at] + lift
+            base[pl.ds(8 * t, 8), at] = gath[pl.ds(8 * t, 8), at] + lift
+        results.append(pltpu.make_async_copy(base.at[:, at], out_hbm.at[:, at], out_sem.at[v]))
+        results[v].start()
 
     for copy in copies[0] + copies[1] + infos:
         copy.wait_send()
     bytes_of(line_all.at[pl.ds(0, n_slab - 1)], send_sem.at[24]).wait()
     bytes_of(mix_all.at[pl.ds(0, n_col - 1)], send_sem.at[25]).wait()
     bytes_of(row_all.at[pl.ds(0, n_slab - 1)], send_sem.at[26]).wait()
+    for result in results:
+        result.wait()
 
 
 def solution(mesh):
@@ -569,7 +588,7 @@
             functools.partial(kernel, n_slab, n_col, centre),
             out_shape=jax.ShapeDtypeStruct((64, NB), F32),
             in_specs=[hbm] * 12,
-            out_specs=pl.BlockSpec(memory_space=pltpu.VMEM),
+            out_specs=hbm,
             scratch_shapes=[
                 vmem((64, NB), F32),
                 vmem((64, NB), F32),
@@ -584,12 +603,14 @@
                 vmem((64, 64), BF16),
                 vmem((n_col, 8, 128), F32),
                 vmem((512, NB), F32),
+                vmem((2, 384, 256), F32),
+                vmem((64, NB), F32),
+                vmem((32, NB), I32),
                 vmem((2, 4, 2, 8, 128), F32),
-                vmem((2, 4, 2, 8, 256), F32),
                 vmem((2, 4, 2, 8, 128), F32),
-                vmem((2, 4, 2, 8, 256), F32),
                 vmem((2, 4, 2, 8, 128), F32),
-                vmem((64, 256), F32),
+                vmem((2, 4, 2, 8, 128), F32),
+                vmem((2, 4, 2, 8, 128), F32),
                 vmem((2, 8, 256), I32),
                 vmem((2, 8, 128), I32),
                 vmem((2, 8, 256), I32),
@@ -604,13 +625,14 @@
                 vmem((1, 128), F32),
                 vmem((n_slab, 1, 128), F32),
                 dma((12,)),
+                dma((4,)),
                 dma((27,)),
                 dma((16,)),
                 dma((8,)),
                 dma,
                 dma,
                 dma,
-                pltpu.SemaphoreType.REGULAR((2,)),
+                pltpu.SemaphoreType.REGULAR((4,)),
             ],
             compiler_params=pltpu.CompilerParams(
                 collective_id=0, has_side_effects=True, vmem_limit_bytes=63 * 1024 * 1024

time: 41.6 us -> 39.9 us (0.959)
  Pallas kernels: 39.9 us -> 38.2 us
    pallas_call x1, Pallas kernels: 39.9 us -> 38.2 us  [shards(): pl.pallas_call(functools.partial(kernel, n_slab, n_col, centre), out_shap...]
where the time goes in v4:
time: 39.9 us; the launch traced here: 39.8 us
  Pallas kernels  38.2 us (96%)
  local copies, waits for them, and re-layouts  1.57 us (4%)
    pallas_call x1, Pallas kernels, shards(): pl.pallas_call(functools.partial(kernel, n_slab, n_col, centre), out_shap...  38.2 us
    unnamed x1, local copies, waits for them, and re-layouts  1.57 us

profile of v4, /device:TPU:1, one launch (start us, length us, event | category | flops | bytes accessed | tf_op | source)
XLA Modules:
  0.0 39.8 jit_solution(11668425760235886395)
XLA Ops:
  0.0 38.2 %shard_map.118 = f32[64,512]{1,0:T(8,128)} custom-call(f32[64,512]{1,0:T(8,128)} %rhs_hbm.1, f32[64,512]{1,0:T(8,128)} %start_hbm.1, f32[64,512]{1,0:T(8,128)} %screen_hbm.1, s32[27,512]{1,0:T(8,128)} %nbr_hbm.1, s32[2,128]{1,0:T(2,128)} %colsend_hbm.1, s32[2,160]{1,0:T(2,128)} %slabsend_hbm.1, s32[1,512]{1,0:T(1,128)} %bitcast.1, f32[2,2,4]{2,1,0:T(2,128)} %coupling_hbm.1, ...), custom_call_target="tpu_custom_call" | custom-call | flops 100000000 | bytes 1000000 | tf_op jit(solution)/shard_map/pallas_call | solution.py:587
  38.2 1.6 %copy.14 = f32[64,512]{1,0:T(8,128)} copy(f32[64,512]{1,0:T(8,128)} %shard_map.118) | data formatting | bytes 262144

commit v5 on v4

--- a/solution.py
+++ b/solution.py
@@ -270,10 +270,6 @@
     for load in loads[6:]:
         load.wait()
 
-    def wait_halo(k):
-        for copy in copies[k]:
-            copy.wait_recv()
-
     def place(there, at):
         return 128 * jnp.where(there, at, AT_NONE)
 
@@ -336,23 +332,25 @@
                         got = jnp.where(masks[w], lanes(gath[pl.ds(8 * t, 8), pl.ds(128 * w, 128)], low), got)
                     gath[pl.ds(64 * blk + 8 * t, 8), pl.ds(128 * v, 128)] = got
 
-    def gather_rims(k, v, slot, half):
+    def gather_rims(k, v, slot, half, along):
         for blk, dx, dy, sz, rows in groups(v):
-            along = (dx == 1 and v == 3) or (dx == -1 and v == 0)
+            if along and not ((dx == 1 and v == 3) or (dx == -1 and v == 0)):
+                continue
             if dy == 0 and not along:
                 continue
             index = pattern(dx, dy, sz, v)
             low, high = index & 127, index >> 7
             for t in rows:
                 a, bh = t // 2, t % 2
-                got = jnp.zeros((8, 128), F32)
-                if dy:
-                    got = jnp.where(high == (AT_CH if dy == 1 else AT_CL), lanes(rc[k, a, bh], low), got)
+                at = (half, pl.ds(64 * (blk - 2) + 8 * t, 8), pl.ds(128 * slot, 128))
+                got = edge[at] if along and dy else jnp.zeros((8, 128), F32)
                 if along:
                     got = jnp.where(high == AT_SLAB, lanes(rs[k, a, bh], low), got)
                     if dy:
                         got = jnp.where(high == (AT_DH if dy == 1 else AT_DL), lanes(diag[k, a, bh], low), got)
-                edge[half, pl.ds(64 * (blk - 2) + 8 * t, 8), pl.ds(128 * slot, 128)] = got
+                else:
+                    got = jnp.where(high == (AT_CH if dy == 1 else AT_CL), lanes(rc[k, a, bh], low), got)
+                edge[at] = got
 
     def product(source, rows):
         high, low = split(source)
@@ -365,15 +363,27 @@
         total = product(gath[...], pl.ds(0, 512))
         base[...] = field + step[...] * (rhs[...] - total - screen[...] * field)
 
-    def sweep_rims(k):
-        for half, vs in ((0, (1, 2)), (1, (0, 3))):
-            for slot, v in enumerate(vs):
-                gather_rims(k, v, slot, half)
-            first = 256 if half == 0 else 128
-            total = product(edge[half, pl.ds(first - 128, 512 - first)], pl.ds(first, 512 - first))
-            for slot, v in enumerate(vs):
-                at = pl.ds(128 * v, 128)
-                gath[pl.ds(0, 64), at] = base[:, at] - step[:, at] * total[:, 128 * slot : 128 * slot + 128]
+    def finish(half, vs):
+        first = 256 if half == 0 else 128
+        total = product(edge[half, pl.ds(first - 128, 512 - first)], pl.ds(first, 512 - first))
+        for slot, v in enumerate(vs):
+            at = pl.ds(128 * v, 128)
+            gath[pl.ds(0, 64), at] = base[:, at] - step[:, at] * total[:, 128 * slot : 128 * slot + 128]
+
+    def sweep_rims(k, meanwhile):
+        for copy in copies[k][6:]:
+            copy.wait_recv()
+        for slot, v in enumerate((1, 2)):
+            gather_rims(k, v, slot, 0, False)
+        finish(0, (1, 2))
+        for slot, v in enumerate((0, 3)):
+            gather_rims(k, v, slot, 1, False)
+        meanwhile()
+        for copy in copies[k][:6]:
+            copy.wait_recv()
+        for slot, v in enumerate((0, 3)):
+            gather_rims(k, v, slot, 1, True)
+        finish(1, (0, 3))
 
     step[...] = RELAX / (centre + screen[...])
     edge[1, pl.ds(0, 128)] = jnp.zeros((128, 256), F32)
@@ -381,18 +391,24 @@
         for v in range(4):
             nbn[pl.ds(8 * r, 8), pl.ds(128 * v, 128)] = place_col(raw_rows(r, v))
     sweep_own()
-    for copy in infos[:2]:
-        copy.wait_recv()
-    for r in range(4):
-        at = (pl.ds(8 * r, 8), pl.ds(0 if r < 2 else 384, 128))
-        nbn[at] = place_slab(raw_rows(r, 0 if r < 2 else 3), nbn[at], r >= 2)
-    wait_halo(0)
-    hear(0)
-    tell(1)
-    if across_far:
-        for d in (2, n_col - 2):
-            pl.semaphore_signal(far_sem.at[3], inc=1, device_id=(s, lax.rem(c + d, n_col)), device_id_type=MESH)
-    sweep_rims(0)
+
+    def after_first():
+        hear(0)
+        tell(1)
+        if across_far:
+            for d in (2, n_col - 2):
+                pl.semaphore_signal(far_sem.at[3], inc=1, device_id=(s, lax.rem(c + d, n_col)), device_id_type=MESH)
+        for copy in infos[:2]:
+            copy.wait_recv()
+        for r in range(4):
+            at = (pl.ds(8 * r, 8), pl.ds(0 if r < 2 else 384, 128))
+            nbn[at] = place_slab(raw_rows(r, 0 if r < 2 else 3), nbn[at], r >= 2)
+
+    def after_second():
+        hear(1)
+        tell(2)
+
+    sweep_rims(0, after_first)
     faces(1)
     copies.append(send_faces(1))
     sweep_own()
@@ -418,10 +434,7 @@
                 code = jnp.where(high == AT_DH, lanes(in_d[side, 0], low) + first + 32, code)
             codes[pl.ds(8 * r, 8), pl.ds(128 * v, 128)] = code
 
-    hear(1)
-    tell(2)
-    wait_halo(1)
-    sweep_rims(1)
+    sweep_rims(1, after_second)
     field = gath[pl.ds(0, 64)]
 
     high, low = split(field)

time: 39.9 us -> 39.3 us (0.985)
  Pallas kernels: 38.2 us -> 37.6 us
    pallas_call x1, Pallas kernels: 38.2 us -> 37.6 us  [shards(): pl.pallas_call(functools.partial(kernel, n_slab, n_col, centre), out_shap...]
where the time goes in v5:
time: 39.3 us; the launch traced here: 39.1 us
  Pallas kernels  37.6 us (96%)
  local copies, waits for them, and re-layouts  1.57 us (4%)
    pallas_call x1, Pallas kernels, shards(): pl.pallas_call(functools.partial(kernel, n_slab, n_col, centre), out_shap...  37.6 us
    unnamed x1, local copies, waits for them, and re-layouts  1.57 us

profile of v5, /device:TPU:1, one launch (start us, length us, event | category | flops | bytes accessed | tf_op | source)
XLA Modules:
  0.0 39.1 jit_solution(9757221243107518767)
XLA Ops:
  0.0 37.6 %shard_map.118 = f32[64,512]{1,0:T(8,128)} custom-call(f32[64,512]{1,0:T(8,128)} %rhs_hbm.1, f32[64,512]{1,0:T(8,128)} %start_hbm.1, f32[64,512]{1,0:T(8,128)} %screen_hbm.1, s32[27,512]{1,0:T(8,128)} %nbr_hbm.1, s32[2,128]{1,0:T(2,128)} %colsend_hbm.1, s32[2,160]{1,0:T(2,128)} %slabsend_hbm.1, s32[1,512]{1,0:T(1,128)} %bitcast.1, f32[2,2,4]{2,1,0:T(2,128)} %coupling_hbm.1, ...), custom_call_target="tpu_custom_call" | custom-call | flops 100000000 | bytes 1000000 | tf_op jit(solution)/shard_map/pallas_call | solution.py:600
  37.6 1.6 %copy.14 = f32[64,512]{1,0:T(8,128)} copy(f32[64,512]{1,0:T(8,128)} %shard_map.118) | data formatting | bytes 262144

commit v6 on v5

--- a/solution.py
+++ b/solution.py
@@ -404,9 +404,47 @@
             at = (pl.ds(8 * r, 8), pl.ds(0 if r < 2 else 384, 128))
             nbn[at] = place_slab(raw_rows(r, 0 if r < 2 else 3), nbn[at], r >= 2)
 
+    reach = {
+        (0, 0): ((0, 1, 2, 3), range(4)),
+        (0, -1): ((0, 1, 2), range(4)),
+        (0, 1): ((0, 1, 2, 3), range(4)),
+        (-1, 0): ((0, 1), (0,)),
+        (-1, -1): ((0,), (0,)),
+        (-1, 1): ((0, 1), (0,)),
+        (1, 0): ((2, 3), (3,)),
+        (1, -1): ((2,), (3,)),
+        (1, 1): ((3,), (3,)),
+    }
+    nought = jnp.zeros((8, 128), F32)
+    held = {(block, k): nought for block in reach for k in range(16)}
+
+    def give(vs):
+        found = {}
+        for v in vs:
+            at = pl.ds(128 * v, 128)
+            field = gath[pl.ds(0, 64), at]
+            high, low = split(field)
+            both = jnp.dot(sums[...], high, preferred_element_type=F32)
+            given = both[:32] + both[32:] + jnp.dot(sums[pl.ds(0, 32)], low, preferred_element_type=F32)
+            local = jnp.sum(rhs[:, at] - screen[:, at] * field, axis=0, keepdims=True)
+            row_at = lax.broadcasted_iota(I32, (32, 128), 0)
+            found[v] = (jnp.where(row_at == 13, jnp.broadcast_to(local, (32, 128)), 0.0) - given) * (1.0 / 64.0)
+        return found
+
+    def tally(found):
+        for (ds, dc), (rs_of, vs_of) in reach.items():
+            for k in range(16):
+                for v in vs_of:
+                    if v in found:
+                        for r in rs_of:
+                            hit = codes[pl.ds(8 * r, 8), pl.ds(128 * v, 128)] == 48 * (ds + 1) + 16 * (dc + 1) + k
+                            part = jnp.where(hit, found[v][8 * r : 8 * r + 8], 0.0)
+                            held[(ds, dc), k] = held[(ds, dc), k] + part
+
     def after_second():
         hear(1)
         tell(2)
+        tally(give((1, 2)))
 
     sweep_rims(0, after_first)
     faces(1)
@@ -435,14 +473,7 @@
             codes[pl.ds(8 * r, 8), pl.ds(128 * v, 128)] = code
 
     sweep_rims(1, after_second)
-    field = gath[pl.ds(0, 64)]
-
-    high, low = split(field)
-    both = jnp.dot(sums[...], high, preferred_element_type=F32)
-    given = both[:32] + both[32:] + jnp.dot(sums[pl.ds(0, 32)], low, preferred_element_type=F32)
-    local = jnp.sum(rhs[...] - screen[...] * field, axis=0, keepdims=True)
-    row_at = lax.broadcasted_iota(I32, (32, 512), 0)
-    given = (jnp.where(row_at == 13, jnp.broadcast_to(local, (32, 512)), 0.0) - given) * (1.0 / 64.0)
+    tally(give((0, 3)))
 
     def fold(parts):
         for bit in (4, 2, 1):
@@ -458,33 +489,12 @@
             parts = merged
         return parts[0]
 
-    reach = {
-        (0, 0): ((0, 1, 2, 3), range(4)),
-        (0, -1): ((0, 1, 2), range(4)),
-        (0, 1): ((0, 1, 2, 3), range(4)),
-        (-1, 0): ((0, 1), (0,)),
-        (-1, -1): ((0,), (0,)),
-        (-1, 1): ((0, 1), (0,)),
-        (1, 0): ((2, 3), (3,)),
-        (1, -1): ((2,), (3,)),
-        (1, 1): ((3,), (3,)),
-    }
-    nought = jnp.zeros((8, 128), F32)
     stacked = []
     for dc in (-1, 0, 1):
         plain, swapped = [], []
         for ds in (-1, 0, 1):
-            rs_of, vs_of = reach[(ds, dc)]
-            first_code = 48 * (ds + 1) + 16 * (dc + 1)
             for x in range(2):
-                parts = []
-                for k in range(8):
-                    acc = nought
-                    for r in rs_of:
-                        for v in vs_of:
-                            hit = codes[pl.ds(8 * r, 8), pl.ds(128 * v, 128)] == first_code + 8 * x + k
-                            acc = acc + jnp.where(hit, given[8 * r : 8 * r + 8, 128 * v : 128 * v + 128], 0.0)
-                    parts.append(acc)
+                parts = [held[(ds, dc), 8 * x + k] for k in range(8)]
                 total = fold(parts)
                 plain.append(total)
                 swapped.append(pltpu.roll(total, 4, 0))

time: 39.3 us -> 39.2 us (level)
  no operation moved by 1% of the time
where the time goes in v6:
time: 39.2 us; the launch traced here: 39 us
  Pallas kernels  37.5 us (96%)
  local copies, waits for them, and re-layouts  1.57 us (4%)
    pallas_call x1, Pallas kernels, shards(): pl.pallas_call(functools.partial(kernel, n_slab, n_col, centre), out_shap...  37.5 us
    unnamed x1, local copies, waits for them, and re-layouts  1.57 us

profile of v6, /device:TPU:1, one launch (start us, length us, event | category | flops | bytes accessed | tf_op | source)
XLA Modules:
  0.0 39.0 jit_solution(858807367655648522)
XLA Ops:
  0.0 37.5 %shard_map.118 = f32[64,512]{1,0:T(8,128)} custom-call(f32[64,512]{1,0:T(8,128)} %rhs_hbm.1, f32[64,512]{1,0:T(8,128)} %start_hbm.1, f32[64,512]{1,0:T(8,128)} %screen_hbm.1, s32[27,512]{1,0:T(8,128)} %nbr_hbm.1, s32[2,128]{1,0:T(2,128)} %colsend_hbm.1, s32[2,160]{1,0:T(2,128)} %slabsend_hbm.1, s32[1,512]{1,0:T(1,128)} %bitcast.1, f32[2,2,4]{2,1,0:T(2,128)} %coupling_hbm.1, ...), custom_call_target="tpu_custom_call" | custom-call | flops 100000000 | bytes 1000000 | tf_op jit(solution)/shard_map/pallas_call | solution.py:610
  37.5 1.6 %copy.14 = f32[64,512]{1,0:T(8,128)} copy(f32[64,512]{1,0:T(8,128)} %shard_map.118) | data formatting | bytes 262144
